TPU v7x, 256 devices: a whole 4x4x8 slice. The times are simulated.
256 devices in a mesh: coil: 8 (over y, x_lo), cuts: 16 (over z, core), frame: 2 (over x_hi).
Axes of the slice: x: 4 (x_hi: 2, x_lo: 2; x = x_hi * 2 + x_lo), y: 4, z: 8, core: 2. Of those that a mesh axis runs over, the one named last changes fastest.
Arguments:
- kspace: bfloat16 [2, 256, 3, 2, 16, 16, 256], P(None, None, None, 'frame', 'cuts', 'coil'), may hold values from -1.5 to 1.5
- coil_maps: bfloat16 [2, 256, 16, 16, 256], P(None, None, 'cuts', 'coil'), may hold values from -0.75 to 0.75
- sampling_masks: int32 [2, 3, 256], P('frame'), may hold values 0 or 1
- start_image: float32 [256, 2, 3, 2, 16, 256], P('coil', None, None, 'frame', 'cuts'), may hold values from -6 to 6
Outputs:
- final_image: float32 [256, 2, 3, 2, 16, 256], P('coil', None, None, 'frame', 'cuts')
- dual_field: float32 [4, 256, 2, 3, 2, 16, 256], P(None, 'coil', None, None, 'frame', 'cuts')
All inputs are finite; a program needn't handle non-finite values. No bound on the sum of `sampling_masks` on one device may be relied on, other than what follows from the above.
Results may differ from a plain program's by a relative error of at most 0.0011.
Values may be sent and summed in bfloat16 or wider, within the bound.
A program may use at most 64 MiB of HBM per device.

v0:
```python
import jax
import jax.numpy as jnp
from jax import lax
from jax.sharding import PartitionSpec as P

OUTER = 2
TV_ITERS = 3


DATA_STEP = 0.5
DUAL_STEP = 0.25
PRIMAL_STEP = 0.25
SMOOTH_WEIGHT = 0.3


def extended(cells, sides, width):
    for axis, dim in sides:
        count = lax.axis_size(axis)
        head = lax.slice_in_dim(cells, 0, width, axis=dim)
        tail = lax.slice_in_dim(cells, cells.shape[dim] - width, cells.shape[dim], axis=dim)
        cells = jnp.concatenate(
            [
                lax.ppermute(tail, axis, [(i, (i + 1) % count) for i in range(count)]),
                cells,
                lax.ppermute(head, axis, [((i + 1) % count, i) for i in range(count)]),
            ],
            axis=dim,
        )
    return cells


def transform_tables(length):
    position = jnp.arange(length, dtype=jnp.int32)
    phase_grid = position[:, None] * position[None, :] % length
    angles = phase_grid.astype(jnp.float32) * (2.0 * jnp.pi / length)
    norming = 1.0 / jnp.sqrt(jnp.asarray(length, jnp.float32))
    real_part = (jnp.cos(angles) * norming).astype(jnp.bfloat16)
    imag_part = (-jnp.sin(angles) * norming).astype(jnp.bfloat16)
    forward_table = jnp.concatenate(
        [jnp.concatenate([real_part, -imag_part], 1), jnp.concatenate([imag_part, real_part], 1)], 0
    )
    adjoint_table = jnp.concatenate(
        [jnp.concatenate([real_part, imag_part], 1), jnp.concatenate([-imag_part, real_part], 1)], 0
    )
    return (forward_table, adjoint_table)


def project(values, complex_dim):
    real_part = lax.index_in_dim(values, 0, complex_dim)
    imag_part = lax.index_in_dim(values, 1, complex_dim)
    magnitude = jnp.sqrt(real_part * real_part + imag_part * imag_part)
    return values / jnp.maximum(magnitude / SMOOTH_WEIGHT, 1.0)


def ahead(field, dim_index):
    length = field.shape[dim_index]
    upper = lax.slice_in_dim(field, 1, length, axis=dim_index)
    padded = jnp.concatenate(
        [upper, jnp.zeros_like(lax.slice_in_dim(field, 0, 1, axis=dim_index))], dim_index
    )
    position = lax.broadcasted_iota(jnp.int32, field.shape, dim_index)
    return jnp.where(position == length - 1, 0.0, padded - field)


def behind(field, dim_index):
    length = field.shape[dim_index]
    lower = lax.slice_in_dim(field, 0, length - 1, axis=dim_index)
    padded = jnp.concatenate(
        [jnp.zeros_like(lax.slice_in_dim(field, 0, 1, axis=dim_index)), lower], dim_index
    )
    return field - padded


def coil_images(rounded, maps_rows):
    picture = rounded.astype(jnp.float32)
    image_real = picture[:, 0][:, :, :, :, None, :]
    image_imag = picture[:, 1][:, :, :, :, None, :]
    map_real = maps_rows[0].astype(jnp.float32)[:, None, None]
    map_imag = maps_rows[1].astype(jnp.float32)[:, None, None]
    return jnp.stack(
        [
            map_real * image_real - map_imag * image_imag,
            map_real * image_imag + map_imag * image_real,
        ]
    ).astype(jnp.bfloat16)


def combine(back_image, maps_rows):
    map_real = maps_rows[0].astype(jnp.float32)[:, None, None]
    map_imag = maps_rows[1].astype(jnp.float32)[:, None, None]
    grad_real = jnp.sum(map_real * back_image[0] + map_imag * back_image[1], axis=4)
    grad_imag = jnp.sum(map_real * back_image[1] - map_imag * back_image[0], axis=4)
    return jnp.stack([grad_real, grad_imag], axis=1)


def shards(kspace, coil_maps, sampling_masks, start_image):
    full_rows = coil_maps.shape[1]
    forward_table, adjoint_table = transform_tables(full_rows)
    mask_base = jnp.transpose(sampling_masks, (2, 1, 0)).astype(jnp.float32)
    mask_rows = mask_base[None, :, :, :, None, None, None]
    first_coil = lax.axis_index("coil") == 0
    last_coil = lax.axis_index("coil") == lax.axis_size("coil") - 1
    first_cut = lax.axis_index("cuts") == 0
    last_cut = lax.axis_index("cuts") == lax.axis_size("cuts") - 1
    current = start_image
    row_edge = jnp.logical_and(
        lax.broadcasted_iota(jnp.int32, current.shape, 0) == current.shape[0] - 1, last_coil
    )
    slice_edge = jnp.logical_and(
        lax.broadcasted_iota(jnp.int32, current.shape, 4) == current.shape[4] - 1, last_cut
    )
    dual_field = jnp.zeros((4,) + current.shape, jnp.float32)
    rim_rows = jnp.zeros_like(current[0:1])
    rim_slices = jnp.zeros_like(current)
    rim_frames = jnp.zeros_like(current)
    for outer_step in range(OUTER):
        rounded = current.astype(jnp.bfloat16)
        coil_data = coil_images(lax.all_gather(rounded, "coil", axis=0, tiled=True), coil_maps)
        spectrum = jnp.dot(
            forward_table, coil_data.reshape(2 * full_rows, -1), preferred_element_type=jnp.float32
        ).reshape(coil_data.shape)
        residual = (mask_rows * (spectrum - kspace.astype(jnp.float32))).astype(jnp.bfloat16)
        flattened = residual.reshape(2 * full_rows, -1)
        row_count = lax.axis_size("coil") * rounded.shape[0]
        upper_rows = lax.slice_in_dim(adjoint_table, 0, row_count, axis=0)
        lower_rows = lax.dynamic_slice_in_dim(adjoint_table, full_rows, row_count, 0)
        back_image = jnp.stack(
            [
                jnp.dot(upper_rows, flattened, preferred_element_type=jnp.float32),
                jnp.dot(lower_rows, flattened, preferred_element_type=jnp.float32),
            ]
        )
        back_image = back_image.reshape((2, row_count) + coil_data.shape[2:])
        anchor = current - DATA_STEP * lax.psum_scatter(
            combine(back_image, coil_maps), "coil", scatter_dimension=0, tiled=True
        )
        primal = anchor
        extrapolated = anchor
        for inner_step in range(TV_ITERS):
            padded = extended(extrapolated, (("coil", 0), ("cuts", 4), ("frame", 3)), 1)
            middle = padded[:, :, :, 1:-1, 1:-1, :]
            row_diff = jnp.where(row_edge, 0.0, middle[2:] - extrapolated)
            col_diff = ahead(extrapolated, 5)
            slice_diff = jnp.where(slice_edge, 0.0, padded[1:-1, :, :, 1:-1, 2:, :] - extrapolated)
            frame_diff = padded[1:-1, :, :, 2:, 1:-1, :] - extrapolated
            dual_field = project(
                dual_field + DUAL_STEP * jnp.stack([row_diff, col_diff, slice_diff, frame_diff]), 2
            )
            rim_rows = jnp.where(
                first_coil,
                0.0,
                project(rim_rows + DUAL_STEP * (extrapolated[0:1] - middle[0:1]), 1),
            )
            rim_slices = jnp.where(
                first_cut,
                0.0,
                project(
                    rim_slices + DUAL_STEP * (extrapolated - padded[1:-1, :, :, 1:-1, 0:1, :]), 1
                ),
            )
            rim_frames = project(
                rim_frames + DUAL_STEP * (extrapolated - padded[1:-1, :, :, 0:1, 1:-1, :]), 1
            )
            spread_sum = (
                dual_field[0]
                - jnp.concatenate([rim_rows, dual_field[0][:-1]], 0)
                + behind(dual_field[1], 5)
            )
            spread_sum = spread_sum + (
                dual_field[2] - jnp.concatenate([rim_slices, dual_field[2][:, :, :, :, :-1]], 4)
            )
            spread_sum = spread_sum + (
                dual_field[3] - jnp.concatenate([rim_frames, dual_field[3][:, :, :, :-1]], 3)
            )
            updated = (primal + PRIMAL_STEP * spread_sum + PRIMAL_STEP * anchor) / (
                1.0 + PRIMAL_STEP
            )
            extrapolated = 2.0 * updated - primal
            primal = updated
        current = primal
    return (current, dual_field)


def solution(mesh):
    return jax.shard_map(
        shards,
        mesh=mesh,
        in_specs=(
            P(None, None, None, "frame", "cuts", "coil", None),
            P(None, None, "cuts", "coil", None),
            P("frame", None, None),
            P("coil", None, None, "frame", "cuts", None),
        ),
        out_specs=(
            P("coil", None, None, "frame", "cuts", None),
            P(None, "coil", None, None, "frame", "cuts", None),
        ),
        check_vma=False,
    )
```

profile of v0, /device:TPU:99, one launch (start us, length us, event | category | flops | bytes accessed | tf_op | source)
XLA Modules:
  0.0 546.7 jit_solution(121345585837814205)
XLA Ops:
  11.0 25.6 %all_gather.6 = bf16[256,2,3,1,1,256]{5,0,4,3,2,1:T(8,128)(2,1)S(1)} all-gather(bf16[32,2,3,1,1,256]{5,0,4,3,2,1:T(8,128)(2,1)S(1)} %copy.330), channel_id=1, replica_groups=mesh['coil'=8,'cuts'=16,'frame'=2] {'coil'}, dimensions={0}, use_global_device_ids=true | all-gather | bytes 884736 | tf_op jit(solution)/shard_map/all_gather | solution.py:118
  39.2 4.6 subtract_convert_fusion.1
  43.8 3.6 pad_maximum_fusion
  52.7 3.9 reshape.2163
  65.6 7.0 %add_reduce_fusion.1 = (f32[256,3,256]{2,1,0:T(4,128)S(1)}, f32[256,3,256]{2,1,0:T(4,128)S(1)}) fusion(f32[256,3,1,1,2,256]{5,4,1,0,3,2:T(2,128)} %squeeze.103, f32[256,3,1,1,2,256]{5,4,1,0,3,2:T(2,128)S(1)} %squeeze.102, f32[256,2,256]{2,1,0:T(2,128)S(1)} %get-tuple-element.29, f32[256,2,256]{2,1,0:T(2,128)S(1)} %get-tuple-element.28), kind=kLoop, calls=%fused_computation.31 | loop fusion | flops 2752512 | bytes 5767168 | tf_op jit(solution)/shard_map/reduce_sum | solution.py:91
  74.3 50.0 %reduce-scatter.3.cloned.1.call-done = f32[32,2,3,1,1,256]{5,0,4,3,2,1:T(8,128)} async-done(((f32[256,2,3,1,1,256]{5,0,4,3,2,1:T(8,128)}), f32[32,2,3,1,1,256]{5,0,4,3,2,1:T(8,128)}) %reduce-scatter.3.cloned.1.call-update) | async-done | bytes 196624 | tf_op jit(solution)/shard_map/reduce_scatter | solution.py:134
  131.3 8.7 %collective-permute-start.3 = (f32[34,2,3,1,1,256]{5,0,2,1,4,3:T(8,128)S(1)}, f32[34,2,3,1,1,256]{5,0,2,1,4,3:T(8,128)S(1)}, u32[]{:S(2)}, u32[]{:S(2)}) collective-permute-start(f32[34,2,3,1,1,256]{5,0,2,1,4,3:T(8,128)S(1)} %pad_maximum_fusion.12), channel_id=1, source_target_pairs={{0,2},{2,4},{4,6},{6,8},{8,10},{10,12},{12,14},{14,16},{16,18},{18... | collective-permute-start | bytes 626696 | tf_op jit(solution)/shard_map/ppermute | solution.py:23
  143.2 3.7 collective-permute-done.2
  150.4 14.6 %collective-permute-done.5 = f32[34,2,3,1,3,256]{5,1,4,3,2,0:T(2,128)S(1)} collective-permute-done((f32[34,2,3,1,3,256]{5,1,4,3,2,0:T(2,128)S(1)}, f32[34,2,3,1,3,256]{5,1,4,3,2,0:T(2,128)S(1)}, u32[]{:S(2)}, u32[]{:S(2)}) %collective-permute-start.5) | collective-permute-done | bytes 626720 | tf_op jit(solution)/shard_map/ppermute | solution.py:23
  165.1 9.9 %collective-permute-done.4 = f32[34,2,3,1,3,256]{5,1,4,3,2,0:T(2,128)S(1)} collective-permute-done((f32[34,2,3,1,3,256]{5,1,4,3,2,0:T(2,128)S(1)}, f32[34,2,3,1,3,256]{5,1,4,3,2,0:T(2,128)S(1)}, u32[]{:S(2)}, u32[]{:S(2)}) %collective-permute-start.4) | collective-permute-done | bytes 626720 | tf_op jit(solution)/shard_map/ppermute | solution.py:25
  179.1 3.6 collective-permute-start.6
  183.5 5.2 collective-permute-start.9
  188.7 3.1 collective-permute-done.9
  191.9 3.8 collective-permute-done.8
  199.4 14.5 %collective-permute-done.10 = f32[34,2,3,1,3,256]{5,1,4,3,2,0:T(2,128)S(1)} collective-permute-done((f32[34,2,3,1,3,256]{5,1,4,3,2,0:T(2,128)S(1)}, f32[34,2,3,1,3,256]{5,1,4,3,2,0:T(2,128)S(1)}, u32[]{:S(2)}, u32[]{:S(2)}) %collective-permute-start.10) | collective-permute-done | bytes 626720 | tf_op jit(solution)/shard_map/ppermute | solution.py:25
  214.8 7.2 %collective-permute-done.11 = f32[34,2,3,1,3,256]{5,1,4,3,2,0:T(2,128)S(1)} collective-permute-done((f32[34,2,3,1,3,256]{5,1,4,3,2,0:T(2,128)S(1)}, f32[34,2,3,1,3,256]{5,1,4,3,2,0:T(2,128)S(1)}, u32[]{:S(2)}, u32[]{:S(2)}) %collective-permute-start.11) | collective-permute-done | bytes 626720 | tf_op jit(solution)/shard_map/ppermute | solution.py:23
  222.6 3.3 collective-permute-done.13
  226.0 3.4 collective-permute-start.12
  230.1 6.5 %collective-permute-start.15 = (f32[34,2,3,1,1,256]{5,0,2,1,4,3:T(8,128)S(1)}, f32[34,2,3,1,1,256]{5,0,2,1,4,3:T(8,128)S(1)}, u32[]{:S(2)}, u32[]{:S(2)}) collective-permute-start(f32[34,2,3,1,1,256]{5,0,2,1,4,3:T(8,128)S(1)} %pad_maximum_fusion.14), channel_id=1, source_target_pairs={{0,2},{2,4},{4,6},{6,8},{8,10},{10,12},{12,14},{14,16},{16,18},{18... | collective-permute-start | bytes 626696 | tf_op jit(solution)/shard_map/ppermute | solution.py:23
  236.7 3.1 collective-permute-done.15
  239.8 3.8 collective-permute-done.14
  247.3 14.5 %collective-permute-done.16 = f32[34,2,3,1,3,256]{5,1,4,3,2,0:T(2,128)S(1)} collective-permute-done((f32[34,2,3,1,3,256]{5,1,4,3,2,0:T(2,128)S(1)}, f32[34,2,3,1,3,256]{5,1,4,3,2,0:T(2,128)S(1)}, u32[]{:S(2)}, u32[]{:S(2)}) %collective-permute-start.16) | collective-permute-done | bytes 626720 | tf_op jit(solution)/shard_map/ppermute | solution.py:25
  263.2 6.7 %collective-permute-done.17 = f32[34,2,3,1,3,256]{5,1,4,3,2,0:T(2,128)S(1)} collective-permute-done((f32[34,2,3,1,3,256]{5,1,4,3,2,0:T(2,128)S(1)}, f32[34,2,3,1,3,256]{5,1,4,3,2,0:T(2,128)S(1)}, u32[]{:S(2)}, u32[]{:S(2)}) %collective-permute-start.17) | collective-permute-done | bytes 626720 | tf_op jit(solution)/shard_map/ppermute | solution.py:23
  271.1 26.7 %all_gather.7 = bf16[256,2,3,1,1,256]{5,0,2,1,4,3:T(8,128)(2,1)S(1)} all-gather(bf16[32,2,3,1,1,256]{5,0,2,1,4,3:T(8,128)(2,1)S(1)} %get-tuple-element.14), channel_id=1, replica_groups=mesh['coil'=8,'cuts'=16,'frame'=2] {'coil'}, dimensions={0}, use_global_device_ids=true | all-gather | bytes 884736 | tf_op jit(solution)/shard_map/all_gather | solution.py:118
  303.8 4.6 subtract_convert_fusion
  308.5 3.6 pad_maximum_fusion.2
  317.5 4.9 reshape.2165
  322.4 3.3 fusion.151
  330.6 3.1 squeeze.117
  333.7 7.2 %add_reduce_fusion = (f32[256,3,256]{2,1,0:T(4,128)S(1)}, f32[256,3,256]{2,1,0:T(4,128)S(1)}) fusion(f32[256,3,1,1,2,256]{5,4,1,0,3,2:T(2,128)} %squeeze.117, f32[256,3,1,1,2,256]{5,4,1,0,3,2:T(2,128)} %squeeze.116, f32[256,2,256]{2,1,0:T(2,128)} %copy-done.4, f32[256,2,256]{2,1,0:T(2,128)} %copy-done.3), kind=kLoop, calls=%fused_computation.27 | loop fusion | flops 2752512 | bytes 5767168 | tf_op jit(solution)/shard_map/reduce_sum | solution.py:91
  342.5 50.6 %reduce-scatter.5.cloned.1.call-done = f32[32,2,3,1,1,256]{5,0,2,1,4,3:T(8,128)} async-done(((f32[256,2,3,1,1,256]{5,0,2,1,4,3:T(8,128)}), f32[32,2,3,1,1,256]{5,0,2,1,4,3:T(8,128)}) %reduce-scatter.5.cloned.1.call-update) | async-done | bytes 196624 | tf_op jit(solution)/shard_map/reduce_scatter | solution.py:134
  400.2 8.7 %collective-permute-start.21 = (f32[34,2,3,1,1,256]{5,0,2,1,4,3:T(8,128)S(1)}, f32[34,2,3,1,1,256]{5,0,2,1,4,3:T(8,128)S(1)}, u32[]{:S(2)}, u32[]{:S(2)}) collective-permute-start(f32[34,2,3,1,1,256]{5,0,2,1,4,3:T(8,128)S(1)} %pad_maximum_fusion.15), channel_id=1, source_target_pairs={{0,2},{2,4},{4,6},{6,8},{8,10},{10,12},{12,14},{14,16},{16,18},{18... | collective-permute-start | bytes 626696 | tf_op jit(solution)/shard_map/ppermute | solution.py:23
  408.9 3.1 collective-permute-done.21
  412.0 3.7 collective-permute-done.20
  419.4 14.5 %collective-permute-done.22 = f32[34,2,3,1,3,256]{5,1,4,3,2,0:T(2,128)S(1)} collective-permute-done((f32[34,2,3,1,3,256]{5,1,4,3,2,0:T(2,128)S(1)}, f32[34,2,3,1,3,256]{5,1,4,3,2,0:T(2,128)S(1)}, u32[]{:S(2)}, u32[]{:S(2)}) %collective-permute-start.22) | collective-permute-done | bytes 626720 | tf_op jit(solution)/shard_map/ppermute | solution.py:25
  435.5 8.4 %collective-permute-done.23 = f32[34,2,3,1,3,256]{5,1,4,3,2,0:T(2,128)S(1)} collective-permute-done((f32[34,2,3,1,3,256]{5,1,4,3,2,0:T(2,128)S(1)}, f32[34,2,3,1,3,256]{5,1,4,3,2,0:T(2,128)S(1)}, u32[]{:S(2)}, u32[]{:S(2)}) %collective-permute-start.23) | collective-permute-done | bytes 626720 | tf_op jit(solution)/shard_map/ppermute | solution.py:23
  447.4 3.6 collective-permute-start.24
  451.9 5.2 collective-permute-start.27
  457.1 3.1 collective-permute-done.27
  460.2 3.8 collective-permute-done.26
  468.0 14.2 %collective-permute-done.28 = f32[34,2,3,1,3,256]{5,1,4,3,2,0:T(2,128)S(1)} collective-permute-done((f32[34,2,3,1,3,256]{5,1,4,3,2,0:T(2,128)S(1)}, f32[34,2,3,1,3,256]{5,1,4,3,2,0:T(2,128)S(1)}, u32[]{:S(2)}, u32[]{:S(2)}) %collective-permute-start.28) | collective-permute-done | bytes 626720 | tf_op jit(solution)/shard_map/ppermute | solution.py:25
  484.1 6.3 %collective-permute-done.29 = f32[34,2,3,1,3,256]{5,1,4,3,2,0:T(2,128)S(1)} collective-permute-done((f32[34,2,3,1,3,256]{5,1,4,3,2,0:T(2,128)S(1)}, f32[34,2,3,1,3,256]{5,1,4,3,2,0:T(2,128)S(1)}, u32[]{:S(2)}, u32[]{:S(2)}) %collective-permute-start.29) | collective-permute-done | bytes 626720 | tf_op jit(solution)/shard_map/ppermute | solution.py:23
  491.0 3.3 collective-permute-done.31
  494.3 3.4 collective-permute-start.30
  498.5 6.6 %collective-permute-start.33 = (f32[34,2,3,1,1,256]{5,0,2,1,4,3:T(8,128)S(1)}, f32[34,2,3,1,1,256]{5,0,2,1,4,3:T(8,128)S(1)}, u32[]{:S(2)}, u32[]{:S(2)}) collective-permute-start(f32[34,2,3,1,1,256]{5,0,2,1,4,3:T(8,128)S(1)} %pad_maximum_fusion.17), channel_id=1, source_target_pairs={{0,2},{2,4},{4,6},{6,8},{8,10},{10,12},{12,14},{14,16},{16,18},{18... | collective-permute-start | bytes 626696 | tf_op jit(solution)/shard_map/ppermute | solution.py:23
  508.2 3.8 collective-permute-done.32
  515.7 14.5 %collective-permute-done.34 = f32[34,2,3,1,3,256]{5,1,4,3,2,0:T(2,128)S(1)} collective-permute-done((f32[34,2,3,1,3,256]{5,1,4,3,2,0:T(2,128)S(1)}, f32[34,2,3,1,3,256]{5,1,4,3,2,0:T(2,128)S(1)}, u32[]{:S(2)}, u32[]{:S(2)}) %collective-permute-start.34) | collective-permute-done | bytes 626720 | tf_op jit(solution)/shard_map/ppermute | solution.py:25
  534.2 4.1 collective-permute-done.35
  (276 shorter events, 106.1 us)
Async XLA Ops:
  7.2 117.1 %reduce-scatter.3.cloned.1.call-start = ((), (), s32[]{:S(2)}) async-start(), calls=%async_computation.2 | async-start | bytes 1769472 | tf_op jit(solution)/shard_map/reduce_scatter | solution.py:134
  8.2 39.6 %copy-start.13 = (bf16[256,256]{1,0:T(8,128)(2,1)}, bf16[256,256]{1,0:T(8,128)(2,1)S(1)}, u32[]{:S(2)}) copy-start(bf16[256,256]{1,0:T(8,128)(2,1)S(1)} %fusion.217) | copy-start | bytes 393220
  9.3 38.5 %copy-start.15 = (bf16[256,256]{1,0:T(8,128)(2,1)}, bf16[256,256]{1,0:T(8,128)(2,1)S(1)}, u32[]{:S(2)}) copy-start(bf16[256,256]{1,0:T(8,128)(2,1)S(1)} %get-tuple-element.71) | copy-start | bytes 393220
  9.3 49.1 %copy-start.7 = (bf16[256,256]{1,0:T(8,128)(2,1)}, bf16[256,256]{1,0:T(8,128)(2,1)S(1)}, u32[]{:S(2)}) copy-start(bf16[256,256]{1,0:T(8,128)(2,1)S(1)} %get-tuple-element.72) | copy-start | bytes 393220
  10.1 37.8 %copy-start.29 = (f32[256,3,1]{0,1,2:T(4,128)}, f32[256,3,1]{0,1,2:T(4,128)S(1)}, u32[]{:S(2)}) copy-start(f32[256,3,1]{0,1,2:T(4,128)S(1)} %copy.340) | copy-start | bytes 9220
  74.2 50.1 %copy-start.23 = (f32[32,2,3,1,1,256]{5,4,3,2,1,0:T(1,128)S(1)}, f32[32,2,3,1,1,256]{5,4,3,2,1,0:T(1,128)}, u32[]{:S(2)}) copy-start(f32[32,2,3,1,1,256]{5,4,3,2,1,0:T(1,128)} %param.7) | copy-start | bytes 589828
  74.2 318.9 %reduce-scatter.5.cloned.1.call-start = ((), (), s32[]{:S(2)}) async-start(), calls=%async_computation.3 | async-start | bytes 1769472 | tf_op jit(solution)/shard_map/reduce_scatter | solution.py:134
  125.3 2.6 collective-permute-start.1
  127.8 3.5 collective-permute-start
  131.3 11.8 %collective-permute-start.3 = (f32[34,2,3,1,1,256]{5,0,2,1,4,3:T(8,128)S(1)}, f32[34,2,3,1,1,256]{5,0,2,1,4,3:T(8,128)S(1)}, u32[]{:S(2)}, u32[]{:S(2)}) collective-permute-start(f32[34,2,3,1,1,256]{5,0,2,1,4,3:T(8,128)S(1)} %pad_maximum_fusion.12), channel_id=1, source_target_pairs={{0,2},{2,4},{4,6},{6,8},{8,10},{10,12},{12,14},{14,16},{16,18},{18... | collective-permute-start | bytes 626696 | tf_op jit(solution)/shard_map/ppermute | solution.py:23
  140.0 6.8 %collective-permute-start.2 = (f32[34,2,3,1,1,256]{5,0,2,1,4,3:T(8,128)S(1)}, f32[34,2,3,1,1,256]{5,0,2,1,4,3:T(8,128)S(1)}, u32[]{:S(2)}, u32[]{:S(2)}) collective-permute-start(f32[34,2,3,1,1,256]{5,0,2,1,4,3:T(8,128)S(1)} %pad_maximum_fusion.12), channel_id=1, source_target_pairs={{2,0},{4,2},{6,4},{8,6},{10,8},{12,10},{14,12},{16,14},{18,16},{20... | collective-permute-start | bytes 626696 | tf_op jit(solution)/shard_map/ppermute | solution.py:25
  140.0 121.8 %copy-start.27 = (pred[256]{0:T(512)(128)(4,1)}, pred[256]{0:T(512)(128)(4,1)S(1)}, u32[]{:S(2)}) copy-start(pred[256]{0:T(512)(128)(4,1)S(1)} %iota_compare_fusion) | copy-start | bytes 772
  147.3 17.8 %collective-permute-start.5 = (f32[34,2,3,1,3,256]{5,1,4,3,2,0:T(2,128)S(1)}, f32[34,2,3,1,3,256]{5,1,4,3,2,0:T(2,128)S(1)}, u32[]{:S(2)}, u32[]{:S(2)}) collective-permute-start(f32[34,2,3,1,3,256]{5,1,4,3,2,0:T(2,128)S(1)} %copy.136), channel_id=1, source_target_pairs={{0,1},{1,0},{2,3},{3,2},{4,5},{5,4},{6,7},{7,6},{8,9},{9,8},{10,11... | collective-permute-start | bytes 1880072 | tf_op jit(solution)/shard_map/ppermute | solution.py:23
  149.2 25.8 %collective-permute-start.4 = (f32[34,2,3,1,3,256]{5,1,4,3,2,0:T(2,128)S(1)}, f32[34,2,3,1,3,256]{5,1,4,3,2,0:T(2,128)S(1)}, u32[]{:S(2)}, u32[]{:S(2)}) collective-permute-start(f32[34,2,3,1,3,256]{5,1,4,3,2,0:T(2,128)S(1)} %copy.136), channel_id=1, source_target_pairs={{1,0},{0,1},{3,2},{2,3},{5,4},{4,5},{7,6},{6,7},{9,8},{8,9},{11,10... | collective-permute-start | bytes 1880072 | tf_op jit(solution)/shard_map/ppermute | solution.py:25
  176.0 3.1 collective-permute-start.7
  179.1 4.4 collective-permute-start.6
  183.5 8.3 %collective-permute-start.9 = (f32[34,2,3,1,1,256]{5,0,2,1,4,3:T(8,128)S(1)}, f32[34,2,3,1,1,256]{5,0,2,1,4,3:T(8,128)S(1)}, u32[]{:S(2)}, u32[]{:S(2)}) collective-permute-start(f32[34,2,3,1,1,256]{5,0,2,1,4,3:T(8,128)S(1)} %pad_maximum_fusion.13), channel_id=1, source_target_pairs={{0,2},{2,4},{4,6},{6,8},{8,10},{10,12},{12,14},{14,16},{16,18},{18... | collective-permute-start | bytes 626696 | tf_op jit(solution)/shard_map/ppermute | solution.py:23
  188.7 7.0 %collective-permute-start.8 = (f32[34,2,3,1,1,256]{5,0,2,1,4,3:T(8,128)S(1)}, f32[34,2,3,1,1,256]{5,0,2,1,4,3:T(8,128)S(1)}, u32[]{:S(2)}, u32[]{:S(2)}) collective-permute-start(f32[34,2,3,1,1,256]{5,0,2,1,4,3:T(8,128)S(1)} %pad_maximum_fusion.13), channel_id=1, source_target_pairs={{2,0},{4,2},{6,4},{8,6},{10,8},{12,10},{14,12},{16,14},{18,16},{20... | collective-permute-start | bytes 626696 | tf_op jit(solution)/shard_map/ppermute | solution.py:25
  196.1 17.8 %collective-permute-start.10 = (f32[34,2,3,1,3,256]{5,1,4,3,2,0:T(2,128)S(1)}, f32[34,2,3,1,3,256]{5,1,4,3,2,0:T(2,128)S(1)}, u32[]{:S(2)}, u32[]{:S(2)}) collective-permute-start(f32[34,2,3,1,3,256]{5,1,4,3,2,0:T(2,128)S(1)} %copy.159), channel_id=1, source_target_pairs={{1,0},{0,1},{3,2},{2,3},{5,4},{4,5},{7,6},{6,7},{9,8},{8,9},{11,10... | collective-permute-start | bytes 1880072 | tf_op jit(solution)/shard_map/ppermute | solution.py:25
  198.3 23.7 %collective-permute-start.11 = (f32[34,2,3,1,3,256]{5,1,4,3,2,0:T(2,128)S(1)}, f32[34,2,3,1,3,256]{5,1,4,3,2,0:T(2,128)S(1)}, u32[]{:S(2)}, u32[]{:S(2)}) collective-permute-start(f32[34,2,3,1,3,256]{5,1,4,3,2,0:T(2,128)S(1)} %copy.159), channel_id=1, source_target_pairs={{0,1},{1,0},{2,3},{3,2},{4,5},{5,4},{6,7},{7,6},{8,9},{9,8},{10,11... | collective-permute-start | bytes 1880072 | tf_op jit(solution)/shard_map/ppermute | solution.py:23
  222.5 3.4 collective-permute-start.13
  226.0 4.1 collective-permute-start.12
  230.1 9.7 %collective-permute-start.15 = (f32[34,2,3,1,1,256]{5,0,2,1,4,3:T(8,128)S(1)}, f32[34,2,3,1,1,256]{5,0,2,1,4,3:T(8,128)S(1)}, u32[]{:S(2)}, u32[]{:S(2)}) collective-permute-start(f32[34,2,3,1,1,256]{5,0,2,1,4,3:T(8,128)S(1)} %pad_maximum_fusion.14), channel_id=1, source_target_pairs={{0,2},{2,4},{4,6},{6,8},{8,10},{10,12},{12,14},{14,16},{16,18},{18... | collective-permute-start | bytes 626696 | tf_op jit(solution)/shard_map/ppermute | solution.py:23
  236.6 7.0 %collective-permute-start.14 = (f32[34,2,3,1,1,256]{5,0,2,1,4,3:T(8,128)S(1)}, f32[34,2,3,1,1,256]{5,0,2,1,4,3:T(8,128)S(1)}, u32[]{:S(2)}, u32[]{:S(2)}) collective-permute-start(f32[34,2,3,1,1,256]{5,0,2,1,4,3:T(8,128)S(1)} %pad_maximum_fusion.14), channel_id=1, source_target_pairs={{2,0},{4,2},{6,4},{8,6},{10,8},{12,10},{14,12},{16,14},{18,16},{20... | collective-permute-start | bytes 626696 | tf_op jit(solution)/shard_map/ppermute | solution.py:25
  244.0 17.8 %collective-permute-start.16 = (f32[34,2,3,1,3,256]{5,1,4,3,2,0:T(2,128)S(1)}, f32[34,2,3,1,3,256]{5,1,4,3,2,0:T(2,128)S(1)}, u32[]{:S(2)}, u32[]{:S(2)}) collective-permute-start(f32[34,2,3,1,3,256]{5,1,4,3,2,0:T(2,128)S(1)} %copy.172), channel_id=1, source_target_pairs={{1,0},{0,1},{3,2},{2,3},{5,4},{4,5},{7,6},{6,7},{9,8},{8,9},{11,10... | collective-permute-start | bytes 1880072 | tf_op jit(solution)/shard_map/ppermute | solution.py:25
  246.3 23.6 %collective-permute-start.17 = (f32[34,2,3,1,3,256]{5,1,4,3,2,0:T(2,128)S(1)}, f32[34,2,3,1,3,256]{5,1,4,3,2,0:T(2,128)S(1)}, u32[]{:S(2)}, u32[]{:S(2)}) collective-permute-start(f32[34,2,3,1,3,256]{5,1,4,3,2,0:T(2,128)S(1)} %copy.172), channel_id=1, source_target_pairs={{0,1},{1,0},{2,3},{3,2},{4,5},{5,4},{6,7},{7,6},{8,9},{9,8},{10,11... | collective-permute-start | bytes 1880072 | tf_op jit(solution)/shard_map/ppermute | solution.py:23
  342.5 50.6 %copy-start.22 = (f32[32,2,3,1,1,256]{5,0,2,1,4,3:T(8,128)S(1)}, f32[32,2,3,1,1,256]{5,0,2,1,4,3:T(8,128)}, u32[]{:S(2)}) copy-start(f32[32,2,3,1,1,256]{5,0,2,1,4,3:T(8,128)} %get-tuple-element.15) | copy-start | bytes 589828
  394.1 2.6 collective-permute-start.19
  396.7 3.5 collective-permute-start.18
  400.2 33.8 %copy-start.10 = (f32[32,2,3,1,1,256]{5,0,2,1,4,3:T(8,128)S(1)}, f32[32,2,3,1,1,256]{5,0,2,1,4,3:T(8,128)}, u32[]{:S(2)}) copy-start(f32[32,2,3,1,1,256]{5,0,2,1,4,3:T(8,128)} %copy-done.9) | copy-start | bytes 589828
  400.2 33.8 %copy-start.19 = (f32[32,3,256]{2,0,1:T(8,128)S(1)}, f32[32,3,256]{2,0,1:T(8,128)}, u32[]{:S(2)}) copy-start(f32[32,3,256]{2,0,1:T(8,128)} %copy-done.18) | copy-start | bytes 294916
  400.2 33.8 %copy-start.28 = (pred[256]{0:T(512)(128)(4,1)S(1)}, pred[256]{0:T(512)(128)(4,1)}, u32[]{:S(2)}) copy-start(pred[256]{0:T(512)(128)(4,1)} %copy-done.27) | copy-start | bytes 772
  400.2 11.8 %collective-permute-start.21 = (f32[34,2,3,1,1,256]{5,0,2,1,4,3:T(8,128)S(1)}, f32[34,2,3,1,1,256]{5,0,2,1,4,3:T(8,128)S(1)}, u32[]{:S(2)}, u32[]{:S(2)}) collective-permute-start(f32[34,2,3,1,1,256]{5,0,2,1,4,3:T(8,128)S(1)} %pad_maximum_fusion.15), channel_id=1, source_target_pairs={{0,2},{2,4},{4,6},{6,8},{8,10},{10,12},{12,14},{14,16},{16,18},{18... | collective-permute-start | bytes 626696 | tf_op jit(solution)/shard_map/ppermute | solution.py:23
  408.9 6.8 %collective-permute-start.20 = (f32[34,2,3,1,1,256]{5,0,2,1,4,3:T(8,128)S(1)}, f32[34,2,3,1,1,256]{5,0,2,1,4,3:T(8,128)S(1)}, u32[]{:S(2)}, u32[]{:S(2)}) collective-permute-start(f32[34,2,3,1,1,256]{5,0,2,1,4,3:T(8,128)S(1)} %pad_maximum_fusion.15), channel_id=1, source_target_pairs={{2,0},{4,2},{6,4},{8,6},{10,8},{12,10},{14,12},{16,14},{18,16},{20... | collective-permute-start | bytes 626696 | tf_op jit(solution)/shard_map/ppermute | solution.py:25
  416.1 17.8 %collective-permute-start.22 = (f32[34,2,3,1,3,256]{5,1,4,3,2,0:T(2,128)S(1)}, f32[34,2,3,1,3,256]{5,1,4,3,2,0:T(2,128)S(1)}, u32[]{:S(2)}, u32[]{:S(2)}) collective-permute-start(f32[34,2,3,1,3,256]{5,1,4,3,2,0:T(2,128)S(1)} %copy.191), channel_id=1, source_target_pairs={{1,0},{0,1},{3,2},{2,3},{5,4},{4,5},{7,6},{6,7},{9,8},{8,9},{11,10... | collective-permute-start | bytes 1880072 | tf_op jit(solution)/shard_map/ppermute | solution.py:25
  418.2 25.7 %collective-permute-start.23 = (f32[34,2,3,1,3,256]{5,1,4,3,2,0:T(2,128)S(1)}, f32[34,2,3,1,3,256]{5,1,4,3,2,0:T(2,128)S(1)}, u32[]{:S(2)}, u32[]{:S(2)}) collective-permute-start(f32[34,2,3,1,3,256]{5,1,4,3,2,0:T(2,128)S(1)} %copy.191), channel_id=1, source_target_pairs={{0,1},{1,0},{2,3},{3,2},{4,5},{5,4},{6,7},{7,6},{8,9},{9,8},{10,11... | collective-permute-start | bytes 1880072 | tf_op jit(solution)/shard_map/ppermute | solution.py:23
  444.3 3.1 collective-permute-start.25
  447.4 4.4 collective-permute-start.24
  451.9 8.3 %collective-permute-start.27 = (f32[34,2,3,1,1,256]{5,0,2,1,4,3:T(8,128)S(1)}, f32[34,2,3,1,1,256]{5,0,2,1,4,3:T(8,128)S(1)}, u32[]{:S(2)}, u32[]{:S(2)}) collective-permute-start(f32[34,2,3,1,1,256]{5,0,2,1,4,3:T(8,128)S(1)} %pad_maximum_fusion.16), channel_id=1, source_target_pairs={{0,2},{2,4},{4,6},{6,8},{8,10},{10,12},{12,14},{14,16},{16,18},{18... | collective-permute-start | bytes 626696 | tf_op jit(solution)/shard_map/ppermute | solution.py:23
  457.1 7.0 %collective-permute-start.26 = (f32[34,2,3,1,1,256]{5,0,2,1,4,3:T(8,128)S(1)}, f32[34,2,3,1,1,256]{5,0,2,1,4,3:T(8,128)S(1)}, u32[]{:S(2)}, u32[]{:S(2)}) collective-permute-start(f32[34,2,3,1,1,256]{5,0,2,1,4,3:T(8,128)S(1)} %pad_maximum_fusion.16), channel_id=1, source_target_pairs={{2,0},{4,2},{6,4},{8,6},{10,8},{12,10},{14,12},{16,14},{18,16},{20... | collective-permute-start | bytes 626696 | tf_op jit(solution)/shard_map/ppermute | solution.py:25
  464.4 17.8 %collective-permute-start.28 = (f32[34,2,3,1,3,256]{5,1,4,3,2,0:T(2,128)S(1)}, f32[34,2,3,1,3,256]{5,1,4,3,2,0:T(2,128)S(1)}, u32[]{:S(2)}, u32[]{:S(2)}) collective-permute-start(f32[34,2,3,1,3,256]{5,1,4,3,2,0:T(2,128)S(1)} %copy.204), channel_id=1, source_target_pairs={{1,0},{0,1},{3,2},{2,3},{5,4},{4,5},{7,6},{6,7},{9,8},{8,9},{11,10... | collective-permute-start | bytes 1880072 | tf_op jit(solution)/shard_map/ppermute | solution.py:25
  466.7 23.7 %collective-permute-start.29 = (f32[34,2,3,1,3,256]{5,1,4,3,2,0:T(2,128)S(1)}, f32[34,2,3,1,3,256]{5,1,4,3,2,0:T(2,128)S(1)}, u32[]{:S(2)}, u32[]{:S(2)}) collective-permute-start(f32[34,2,3,1,3,256]{5,1,4,3,2,0:T(2,128)S(1)} %copy.204), channel_id=1, source_target_pairs={{0,1},{1,0},{2,3},{3,2},{4,5},{5,4},{6,7},{7,6},{8,9},{9,8},{10,11... | collective-permute-start | bytes 1880072 | tf_op jit(solution)/shard_map/ppermute | solution.py:23
  490.9 3.4 collective-permute-start.31
  494.3 4.1 collective-permute-start.30
  498.5 9.7 %collective-permute-start.33 = (f32[34,2,3,1,1,256]{5,0,2,1,4,3:T(8,128)S(1)}, f32[34,2,3,1,1,256]{5,0,2,1,4,3:T(8,128)S(1)}, u32[]{:S(2)}, u32[]{:S(2)}) collective-permute-start(f32[34,2,3,1,1,256]{5,0,2,1,4,3:T(8,128)S(1)} %pad_maximum_fusion.17), channel_id=1, source_target_pairs={{0,2},{2,4},{4,6},{6,8},{8,10},{10,12},{12,14},{14,16},{16,18},{18... | collective-permute-start | bytes 626696 | tf_op jit(solution)/shard_map/ppermute | solution.py:23
  505.0 7.0 %collective-permute-start.32 = (f32[34,2,3,1,1,256]{5,0,2,1,4,3:T(8,128)S(1)}, f32[34,2,3,1,1,256]{5,0,2,1,4,3:T(8,128)S(1)}, u32[]{:S(2)}, u32[]{:S(2)}) collective-permute-start(f32[34,2,3,1,1,256]{5,0,2,1,4,3:T(8,128)S(1)} %pad_maximum_fusion.17), channel_id=1, source_target_pairs={{2,0},{4,2},{6,4},{8,6},{10,8},{12,10},{14,12},{16,14},{18,16},{20... | collective-permute-start | bytes 626696 | tf_op jit(solution)/shard_map/ppermute | solution.py:25
  512.4 17.8 %collective-permute-start.34 = (f32[34,2,3,1,3,256]{5,1,4,3,2,0:T(2,128)S(1)}, f32[34,2,3,1,3,256]{5,1,4,3,2,0:T(2,128)S(1)}, u32[]{:S(2)}, u32[]{:S(2)}) collective-permute-start(f32[34,2,3,1,3,256]{5,1,4,3,2,0:T(2,128)S(1)} %copy.227), channel_id=1, source_target_pairs={{1,0},{0,1},{3,2},{2,3},{5,4},{4,5},{7,6},{6,7},{9,8},{8,9},{11,10... | collective-permute-start | bytes 1880072 | tf_op jit(solution)/shard_map/ppermute | solution.py:25
  514.5 23.8 %collective-permute-start.35 = (f32[34,2,3,1,3,256]{5,1,4,3,2,0:T(2,128)S(1)}, f32[34,2,3,1,3,256]{5,1,4,3,2,0:T(2,128)S(1)}, u32[]{:S(2)}, u32[]{:S(2)}) collective-permute-start(f32[34,2,3,1,3,256]{5,1,4,3,2,0:T(2,128)S(1)} %copy.227), channel_id=1, source_target_pairs={{0,1},{1,0},{2,3},{3,2},{4,5},{5,4},{6,7},{7,6},{8,9},{9,8},{10,11... | collective-permute-start | bytes 1880072 | tf_op jit(solution)/shard_map/ppermute | solution.py:23
  (23 other events, 162.5 us)
Sparse Core Ops, SparseCore 0:
  74.3 49.9 reduce-scatter.2
  342.6 50.4 reduce-scatter.4
where the time goes:
time: 555 us; the launch traced here: 547 us
  waiting for transfers between devices  292 us (53%)
  starting transfers between devices  81.5 us (15%)
  blocking collectives  52.3 us (9%)
  other arithmetic  50.4 us (9%)
  local copies, waits for them, and re-layouts  44.4 us (8%)
  between operations  15.7 us (3%)
  matrix products  10.6 us (2%)
    ppermute x18, waiting for transfers between devices, extended(): lax.ppermute(head, axis, [((i + 1) % count, i) for i in range(count)])  109 us
    reduce_scatter x2, waiting for transfers between devices, shards(): lax.psum_scatter(combine(back_image, coil_maps), 'coil', scatter_dimensio...  101 us
    ppermute x18, waiting for transfers between devices, extended(): lax.ppermute(tail, axis, [(i, (i + 1) % count) for i in range(count)])  81.8 us
    all_gather x2, blocking collectives, shards(): lax.all_gather(rounded, 'coil', axis=0, tiled=True)  52.3 us
    ppermute x18, starting transfers between devices, extended(): lax.ppermute(tail, axis, [(i, (i + 1) % count) for i in range(count)])  50.8 us
    ppermute x18, starting transfers between devices, extended(): lax.ppermute(head, axis, [((i + 1) % count, i) for i in range(count)])  30.6 us
    reduce_sum x2, other arithmetic, combine(): jnp.sum(map_real * back_image[0] + map_imag * back_image[1], axis=4)  14.2 us
  transfers between devices with their start and end apart: 38, of which 38 were waited for; matrix products, arithmetic and copies ran while one was open for 2% of the time, Pallas kernels for 0%

commit v1 on v0

v1 whole, which is shorter than its diff:
```python
import functools

import jax
import jax.numpy as jnp
import ml_dtypes
import numpy as np
from jax import lax
from jax.experimental import pallas as pl
from jax.experimental.pallas import tpu as pltpu
from jax.sharding import PartitionSpec as P

OUTER = 2
TV_ITERS = 3
STAGES = TV_ITERS + 2

DATA_STEP = 0.5
DUAL_STEP = 0.25
PRIMAL_STEP = 0.25
SMOOTH_WEIGHT = 0.3

MESH = pl.DeviceIdType.MESH
BF16 = jnp.bfloat16
F32 = jnp.float32


def transform_tables(length):
    position = np.arange(length, dtype=np.int64)
    phase_grid = (position[:, None] * position[None, :]) % length
    angles = phase_grid.astype(np.float32) * np.float32(2.0 * np.pi / length)
    norming = np.float32(1.0) / np.sqrt(np.float32(length))
    real_part = (np.cos(angles) * norming).astype(ml_dtypes.bfloat16)
    imag_part = (-np.sin(angles) * norming).astype(ml_dtypes.bfloat16)
    forward_table = np.block([[real_part, -imag_part], [imag_part, real_part]])
    adjoint_table = np.block([[real_part, imag_part], [-imag_part, real_part]])
    return forward_table, adjoint_table


def project(real_part, imag_part):
    factor = jnp.minimum(
        SMOOTH_WEIGHT * lax.rsqrt(real_part * real_part + imag_part * imag_part), 1.0
    )
    return real_part * factor, imag_part * factor


def kernel(
    sizes,
    kspace_hbm, maps_hbm, mask_ref, image_hbm, forward_hbm, adjoint_hbm,
    image_out, dual_out,
    kspace_raw, maps_raw, kspace_ref, maps_ref, forward_ref, adjoint_ref, masked_ref,
    gathered, coil_data, residual, partial, arrived,
    primal, anchor, bar, dual, rim_rows, rim_slices, halo_rows, halo_wide,
    load_sem, ag_send, ag_recv, rs_send, rs_recv, halo_send, halo_recv, out_sem,
):
    NR, NCOL, NC, ENC, COIL, CUTS, FRAME = sizes
    ROWS = NR // COIL
    me = lax.axis_index("coil")
    cut = lax.axis_index("cuts")
    frame = lax.axis_index("frame")
    my_rows = pl.ds(pl.multiple_of(me * ROWS, ROWS), ROWS)

    peers = [{"coil": lax.rem(me + d, COIL)} for d in range(1, COIL)]
    above, below = {"coil": lax.rem(me + COIL - 1, COIL)}, {"coil": lax.rem(me + 1, COIL)}
    before, behind = {"cuts": lax.rem(cut + CUTS - 1, CUTS)}, {"cuts": lax.rem(cut + 1, CUTS)}
    partner = {"frame": 1 - frame}

    def image_load(e, p):
        return pltpu.make_async_copy(
            image_hbm.at[:, p * ENC + e, 0, :], primal.at[e, p], load_sem.at[2 * e + p]
        )

    def plain_load(src, dst, i):
        return pltpu.make_async_copy(src, dst, load_sem.at[2 * ENC + i])

    loads = [
        plain_load(maps_hbm, maps_raw, 0),
        plain_load(forward_hbm, forward_ref, 1),
        plain_load(kspace_hbm, kspace_raw, 2),
        plain_load(adjoint_hbm, adjoint_ref, 3),
    ]
    for e in range(ENC):
        for p in range(2):
            image_load(e, p).start()
    for load in loads:
        load.start()

    barrier = pltpu.get_barrier_semaphore()
    greeted = peers + [before, behind, partner]
    for other in greeted:
        pl.semaphore_signal(barrier, inc=1, device_id=other, device_id_type=MESH)
    pl.semaphore_wait(barrier, len(greeted))

    def ag_copy(e, d):
        return pltpu.make_async_remote_copy(
            gathered.at[e, :, my_rows, :], gathered.at[e, :, my_rows, :],
            ag_send.at[e, d], ag_recv.at[e, d], device_id=peers[d], device_id_type=MESH,
        )

    def ag_wait(e, d):
        rows = pl.ds(pl.multiple_of(lax.rem(me + COIL - 1 - d, COIL) * ROWS, ROWS), ROWS)
        here = gathered.at[e, :, rows, :]
        pltpu.make_async_remote_copy(
            here, here, ag_send.at[e, d], ag_recv.at[e, d], device_id=peers[d], device_id_type=MESH
        ).wait_recv()

    def rs_copy(e, d):
        return pltpu.make_async_remote_copy(
            partial.at[e, peers[d]["coil"]], arrived.at[e, d],
            rs_send.at[e, d], rs_recv.at[e, d], device_id=peers[d], device_id_type=MESH,
        )

    def halo_copies(e, parity):
        plan = [
            (bar.at[e, :, pl.ds(ROWS - 8, 8), :], halo_rows.at[parity, e, 0], below),
            (bar.at[e, :, pl.ds(0, 8), :], halo_rows.at[parity, e, 1], above),
            (bar.at[e], halo_wide.at[parity, e, 0], behind),
            (bar.at[e], halo_wide.at[parity, e, 1], before),
            (bar.at[e], halo_wide.at[parity, e, 2], partner),
        ]
        return [
            pltpu.make_async_remote_copy(
                src, dst, halo_send.at[e, i], halo_recv.at[parity, e, i],
                device_id=to, device_id_type=MESH,
            )
            for i, (src, dst, to) in enumerate(plan)
        ]

    def out_copies(e):
        copies = []
        for p in range(2):
            copies.append((primal.at[e, p], image_out.at[:, p * ENC + e, 0, :]))
            for k in range(4):
                copies.append((dual.at[e, k, p], dual_out.at[k, :, p * ENC + e, 0, :]))
        return [
            pltpu.make_async_copy(src, dst, out_sem.at[e, i]) for i, (src, dst) in enumerate(copies)
        ]

    def send_rounded(e):
        for p in range(2):
            gathered[e, p, my_rows, :] = primal[e, p].astype(BF16)
        for d in range(COIL - 1):
            ag_copy(e, d).start()

    for e in range(ENC):
        for p in range(2):
            image_load(e, p).wait()
        send_rounded(e)

    row_id = lax.broadcasted_iota(jnp.int32, (256, 256), 0)
    col_id = lax.broadcasted_iota(jnp.int32, (256, 256), 1)
    source = jnp.where(row_id < 128, 2 * row_id, 2 * row_id - 255)
    sort_rows = jnp.where(col_id == source, 1.0, 0.0).astype(BF16)

    def sorted_pair(block):
        return jnp.dot(
            sort_rows, block.reshape(256, NCOL), preferred_element_type=F32
        ).astype(BF16)

    loads[0].wait()
    for p in range(2):
        def maps_part(i, carry):
            rows = pl.ds(pl.multiple_of(i * 128, 128), 128)
            both = sorted_pair(maps_raw[p, rows])
            maps_ref[p, 0, rows, :] = both[:128]
            maps_ref[p, 1, rows, :] = both[128:]
            return carry

        lax.fori_loop(0, NR // 128, maps_part, 0)
    loads[2].wait()
    for p in range(2):
        def kspace_part(i, carry):
            e, part = lax.rem(i, ENC), lax.div(i, ENC)
            rows = pl.ds(pl.multiple_of(part * 128, 128), 128)
            both = sorted_pair(kspace_raw[p, rows, e])
            kspace_ref[e, p, 0, rows, :] = both[:128]
            kspace_ref[e, p, 1, rows, :] = both[128:]
            return carry

        lax.fori_loop(0, ENC * NR // 128, kspace_part, 0)
    loads[3].wait()
    for e in range(ENC):
        sampled = mask_ref[e].astype(F32)
        masked_ref[e] = (adjoint_ref[...].astype(F32) * sampled).astype(BF16)
    dual[...] = jnp.zeros_like(dual)
    rim_rows[...] = jnp.zeros_like(rim_rows)
    rim_slices[...] = jnp.zeros_like(rim_slices)
    loads[1].wait()

    def data_stage(e):
        for d in range(COIL - 1):
            ag_wait(e, d)
        for c in range(NC):
            map_real, map_imag = maps_ref[0, c].astype(F32), maps_ref[1, c].astype(F32)
            image_real, image_imag = gathered[e, 0].astype(F32), gathered[e, 1].astype(F32)
            coil_data[c, :NR] = (map_real * image_real - map_imag * image_imag).astype(BF16)
            coil_data[c, NR:] = (map_real * image_imag + map_imag * image_real).astype(BF16)
            for p in range(2):
                spectrum = jnp.dot(
                    forward_ref[p * NR : (p + 1) * NR], coil_data[c], preferred_element_type=F32
                )
                residual[c, p * NR : (p + 1) * NR] = (
                    spectrum - kspace_ref[e, p, c].astype(F32)
                ).astype(BF16)
        for c in range(NC):
            map_real, map_imag = maps_ref[0, c].astype(F32), maps_ref[1, c].astype(F32)
            back_real = jnp.dot(masked_ref[e, :NR], residual[c], preferred_element_type=F32)
            back_imag = jnp.dot(masked_ref[e, NR:], residual[c], preferred_element_type=F32)
            grad_real = (map_real * back_real + map_imag * back_imag).reshape(COIL, ROWS, NCOL)
            grad_imag = (map_real * back_imag - map_imag * back_real).reshape(COIL, ROWS, NCOL)
            if c == 0:
                partial[e, :, 0], partial[e, :, 1] = grad_real, grad_imag
            else:
                partial[e, :, 0] += grad_real
                partial[e, :, 1] += grad_imag
        for d in range(COIL - 1):
            rs_copy(e, d).start()
        for d in range(COIL - 1):
            ag_copy(e, d).wait_send()

    def anchor_stage(e, turn):
        for d in range(COIL - 1):
            rs_copy(e, d).wait_recv()
        for p in range(2):
            total = partial[e, me, p]
            for d in range(COIL - 1):
                total = total + arrived[e, d, p]
            moved = primal[e, p] - DATA_STEP * total
            anchor[e, p] = moved
            primal[e, p] = moved
            bar[e, p] = moved
        for copy in halo_copies(e, lax.rem(turn, 2)):
            copy.start()
        for d in range(COIL - 1):
            rs_copy(e, d).wait_send()

    rows_at = lax.broadcasted_iota(jnp.int32, (ROWS, NCOL), 0)
    cols_at = lax.broadcasted_iota(jnp.int32, (ROWS, NCOL), 1)
    last_row = rows_at == ROWS - 1
    first_row = rows_at == 0
    row_keep = jnp.where(jnp.logical_and(last_row, me == COIL - 1), 0.0, DUAL_STEP)
    rim_keep = jnp.where(me == 0, 0.0, 1.0)
    slice_keep = jnp.where(cut == CUTS - 1, 0.0, DUAL_STEP)
    rim_slice_keep = jnp.where(cut == 0, 0.0, 1.0)
    col_keep = jnp.where(cols_at == NCOL - 1, 0.0, DUAL_STEP)
    col_back = jnp.where(cols_at == 0, 0.0, 1.0)

    def tv_stage(e, it, outer):
        parity = lax.rem(outer * TV_ITERS + it, 2)
        for copy in halo_copies(e, parity):
            copy.wait_recv()
        for copy in halo_copies(e, parity):
            copy.wait_send()
        x = [bar[e, p] for p in range(2)]
        spread = [None, None]

        def stepped(k, diffs):
            new = project(*[dual[e, k, p] + diffs[p] for p in range(2)])
            for p in range(2):
                dual[e, k, p] = new[p]
            return new

        rows = stepped(0, [
            row_keep * (jnp.where(last_row, halo_rows[parity, e, 1, p, 0:1, :], pltpu.roll(x[p], ROWS - 1, 0)) - x[p])
            for p in range(2)
        ])
        rim = project(*[
            rim_rows[e, p] + DUAL_STEP * (x[p][0:8] - halo_rows[parity, e, 0, p, 7:8, :])
            for p in range(2)
        ])
        for p in range(2):
            edge = rim[p] * rim_keep
            rim_rows[e, p] = edge
            spread[p] = rows[p] - jnp.where(first_row, edge[0:1], pltpu.roll(rows[p], 1, 0))
        cols = stepped(1, [col_keep * (pltpu.roll(x[p], NCOL - 1, 1) - x[p]) for p in range(2)])
        for p in range(2):
            spread[p] = spread[p] + (cols[p] - col_back * pltpu.roll(cols[p], 1, 1))
        cuts = stepped(2, [slice_keep * (halo_wide[parity, e, 1, p] - x[p]) for p in range(2)])
        rim = project(*[
            rim_slices[e, p] + DUAL_STEP * (x[p] - halo_wide[parity, e, 0, p]) for p in range(2)
        ])
        for p in range(2):
            edge = rim[p] * rim_slice_keep
            rim_slices[e, p] = edge
            spread[p] = spread[p] + (cuts[p] - edge)
        frames = stepped(3, [DUAL_STEP * (halo_wide[parity, e, 2, p] - x[p]) for p in range(2)])
        for p in range(2):
            spread[p] = spread[p] + 2.0 * frames[p]
            held = primal[e, p]
            updated = (held + PRIMAL_STEP * spread[p] + PRIMAL_STEP * anchor[e, p]) * (
                1.0 / (1.0 + PRIMAL_STEP)
            )
            primal[e, p] = updated
            bar[e, p] = 2.0 * updated - held

        @pl.when(it < TV_ITERS - 1)
        def _():
            for copy in halo_copies(e, 1 - parity):
                copy.start()

        @pl.when(jnp.logical_and(it == TV_ITERS - 1, outer < OUTER - 1))
        def _():
            send_rounded(e)

        @pl.when(jnp.logical_and(it == TV_ITERS - 1, outer == OUTER - 1))
        def _():
            for copy in out_copies(e):
                copy.start()

    def slot(t, carry):
        def one(i, carry):
            e = ENC - 1 - i
            at = t - e
            outer = lax.div(at, STAGES)
            stage = lax.rem(at, STAGES)
            active = jnp.logical_and(at >= 0, at < OUTER * STAGES)

            @pl.when(jnp.logical_and(active, stage == 0))
            def _():
                data_stage(e)

            @pl.when(jnp.logical_and(active, stage == 1))
            def _():
                anchor_stage(e, outer * TV_ITERS)

            @pl.when(jnp.logical_and(active, stage >= 2))
            def _():
                tv_stage(e, stage - 2, outer)

            return carry

        return lax.fori_loop(0, ENC, one, carry)

    lax.fori_loop(0, OUTER * STAGES + ENC - 1, slot, 0)

    for e in range(ENC):
        for copy in out_copies(e):
            copy.wait()


def solution(mesh):
    COIL, CUTS, FRAME = mesh.shape["coil"], mesh.shape["cuts"], mesh.shape["frame"]

    def shards(kspace, coil_maps, sampling_masks, start_image):
        _, NR, ENC, _, _, NC, NCOL = kspace.shape
        ROWS = start_image.shape[0]
        forward_table, adjoint_table = transform_tables(NR)
        masks = jnp.concatenate([sampling_masks[0], sampling_masks[0]], axis=-1)[:, None, :]
        hbm = pl.BlockSpec(memory_space=pltpu.HBM)
        vmem = pl.BlockSpec(memory_space=pltpu.VMEM)
        dma = pltpu.SemaphoreType.DMA
        image, dual = pl.pallas_call(
            functools.partial(kernel, (NR, NCOL, NC, ENC, COIL, CUTS, FRAME)),
            out_shape=(
                jax.ShapeDtypeStruct((ROWS, 2 * ENC, 1, NCOL), F32),
                jax.ShapeDtypeStruct((4, ROWS, 2 * ENC, 1, NCOL), F32),
            ),
            in_specs=[hbm, hbm, vmem, hbm, hbm, hbm],
            out_specs=(hbm, hbm),
            scratch_shapes=[
                pltpu.VMEM((2, NR, ENC, NC, NCOL), BF16),
                pltpu.VMEM((2, NR, NC, NCOL), BF16),
                pltpu.VMEM((ENC, 2, NC, NR, NCOL), BF16),
                pltpu.VMEM((2, NC, NR, NCOL), BF16),
                pltpu.VMEM((2 * NR, 2 * NR), BF16),
                pltpu.VMEM((2 * NR, 2 * NR), BF16),
                pltpu.VMEM((ENC, 2 * NR, 2 * NR), BF16),
                pltpu.VMEM((ENC, 2, NR, NCOL), BF16),
                pltpu.VMEM((NC, 2 * NR, NCOL), BF16),
                pltpu.VMEM((NC, 2 * NR, NCOL), BF16),
                pltpu.VMEM((ENC, COIL, 2, ROWS, NCOL), F32),
                pltpu.VMEM((ENC, COIL - 1, 2, ROWS, NCOL), F32),
                pltpu.VMEM((ENC, 2, ROWS, NCOL), F32),
                pltpu.VMEM((ENC, 2, ROWS, NCOL), F32),
                pltpu.VMEM((ENC, 2, ROWS, NCOL), F32),
                pltpu.VMEM((ENC, 4, 2, ROWS, NCOL), F32),
                pltpu.VMEM((ENC, 2, 8, NCOL), F32),
                pltpu.VMEM((ENC, 2, ROWS, NCOL), F32),
                pltpu.VMEM((2, ENC, 2, 2, 8, NCOL), F32),
                pltpu.VMEM((2, ENC, 3, 2, ROWS, NCOL), F32),
                dma((2 * ENC + 4,)),
                dma((ENC, COIL - 1)),
                dma((ENC, COIL - 1)),
                dma((ENC, COIL - 1)),
                dma((ENC, COIL - 1)),
                dma((ENC, 5)),
                dma((2, ENC, 5)),
                dma((ENC, 10)),
            ],
            compiler_params=pltpu.CompilerParams(
                collective_id=0, has_side_effects=True, vmem_limit_bytes=40 << 20
            ),
            name="sense_tv",
        )(
            kspace.reshape(2, NR, ENC, NC, NCOL),
            coil_maps.reshape(2, NR, NC, NCOL),
            masks,
            start_image.reshape(ROWS, 2 * ENC, 1, NCOL),
            jnp.asarray(forward_table),
            jnp.asarray(adjoint_table),
        )
        return (
            image.reshape(ROWS, 2, ENC, 1, 1, NCOL),
            dual.reshape(4, ROWS, 2, ENC, 1, 1, NCOL),
        )

    return jax.shard_map(
        shards,
        mesh=mesh,
        in_specs=(
            P(None, None, None, "frame", "cuts", "coil", None),
            P(None, None, "cuts", "coil", None),
            P("frame", None, None),
            P("coil", None, None, "frame", "cuts", None),
        ),
        out_specs=(
            P("coil", None, None, "frame", "cuts", None),
            P(None, "coil", None, None, "frame", "cuts", None),
        ),
        check_vma=False,
    )
```

time: 555 us -> 109 us (0.20); the launches traced: 547 us -> 108 us
  waiting for transfers between devices: 292 us -> 0 us
  Pallas kernels: 0 us -> 99.5 us
  starting transfers between devices: 81.5 us -> 0 us
  blocking collectives: 52.3 us -> 0 us
  other arithmetic: 50.4 us -> 0.01 us
  local copies, waits for them, and re-layouts: 44.4 us -> 7.7 us
  between operations: 15.7 us -> 0.65 us
  matrix products: 10.6 us -> 0 us
    ppermute x36 -> x0, waiting for transfers between devices: 191 us -> none  [the longest x18 109 us: extended(): lax.ppermute(head, axis, [((i + 1) % count, i) for i in range(count)])]
    reduce_scatter x2 -> x0, waiting for transfers between devices: 101 us -> none  [shards(): lax.psum_scatter(combine(back_image, coil_maps), 'coil', scatter_dimensio...]
    pallas_call x0 -> x1, Pallas kernels: none -> 99.5 us  [shards(): pl.pallas_call(functools.partial(kernel, (NR, NCOL, NC, ENC, COIL, CUTS,...]
    ppermute x36 -> x0, starting transfers between devices: 81.4 us -> none  [the longest x18 50.8 us: extended(): lax.ppermute(tail, axis, [(i, (i + 1) % count) for i in range(count)])]
    all_gather x2 -> x0, blocking collectives: 52.3 us -> none  [shards(): lax.all_gather(rounded, 'coil', axis=0, tiled=True)]
    another operation x8 -> x0, other arithmetic: 19.2 us -> none
    reduce_sum x2 -> x0, other arithmetic: 14.2 us -> none  [combine(): jnp.sum(map_real * back_image[0] + map_imag * back_image[1], axis=4)]
    squeeze x10 -> x0, local copies, waits for them, and re-layouts: 11.7 us -> none  [the longest x2 6.2 us: combine(): back_image[1]]
  transfers between devices with their start and end apart: 38 -> 0, of which waited for: 38 -> 0; matrix products, arithmetic and copies ran while one was open for 2% -> 0% of each run, Pallas kernels for 0% -> 0%
where the time goes in v1:
time: 109 us; the launch traced here: 108 us
  Pallas kernels  99.5 us (91%)
  local copies, waits for them, and re-layouts  7.7 us (7%)
    pallas_call x1, Pallas kernels, shards(): pl.pallas_call(functools.partial(kernel, (NR, NCOL, NC, ENC, COIL, CUTS,...  99.5 us
    unnamed x13, local copies, waits for them, and re-layouts  7.7 us

profile of v1, /device:TPU:99, one launch (start us, length us, event | category | flops | bytes accessed | tf_op | source)
XLA Modules:
  0.0 107.8 jit_solution(2473092272629400865)
XLA Ops:
  0.6 0.7 copy.12
  1.3 0.0 copy-start
  1.3 1.4 %copy-done = bf16[2,256,3,1,1,2,256]{6,5,4,3,2,1,0:T(2,128)(2,1)S(1)} copy-done((bf16[2,256,3,1,1,2,256]{6,5,4,3,2,1,0:T(2,128)(2,1)S(1)}, bf16[2,256,3,1,1,2,256]{6,5,4,3,2,1,0:T(2,128)(2,1)}, u32[]{:S(2)}) %copy-start) | copy-done | bytes 1572888
  2.7 0.0 copy-start.1
  2.7 1.0 copy-done.1
  3.8 0.0 copy-start.2
  3.8 1.0 copy-done.2
  4.8 0.0 copy-start.3
  4.8 1.0 copy-done.3
  5.9 0.0 copy-start.4
  5.9 0.9 copy-done.4
  6.8 99.5 %sense_tv.1 = (f32[32,6,1,256]{3,2,1,0:T(1,128)S(1)}, f32[4,32,6,1,256]{4,3,2,1,0:T(1,128)S(1)}) custom-call(bf16[2,256,3,2,256]{4,3,2,1,0:T(2,128)(2,1)S(1)} %bitcast.12, bf16[2,256,2,256]{3,2,1,0:T(2,128)(2,1)S(1)} %bitcast.14, s32[3,1,512]{2,1,0:T(1,128)S(1)} %broadcast_in_dim.3.mask_ref, f32[32,6,1,256]{3,2,1,0:T(1,128)S(1)} %bitcast.15, ...), custom_call_target="tpu_custom_call" | custom-call | tf_op jit(solution)/shard_map/sense_tv/pallas_call | solution.py:350
  106.3 0.7 copy.15
  107.0 0.9 copy.16
  (2 shorter events, 0.0 us)
Async XLA Ops:
  1.3 1.4 %copy-start = (bf16[2,256,3,1,1,2,256]{6,5,4,3,2,1,0:T(2,128)(2,1)S(1)}, bf16[2,256,3,1,1,2,256]{6,5,4,3,2,1,0:T(2,128)(2,1)}, u32[]{:S(2)}) copy-start(bf16[2,256,3,1,1,2,256]{6,5,4,3,2,1,0:T(2,128)(2,1)} %param.6) | copy-start | bytes 4718596
  2.7 1.0 copy-start.1
  3.8 1.0 copy-start.2
  4.8 1.0 copy-start.3
  5.9 0.9 copy-start.4

commit v2 on v1

v2 whole, which is shorter than its diff:
```python
import functools

import jax
import jax.numpy as jnp
import ml_dtypes
import numpy as np
from jax import lax
from jax.experimental import pallas as pl
from jax.experimental.pallas import tpu as pltpu
from jax.sharding import PartitionSpec as P

OUTER = 2
TV_ITERS = 3
STAGES = TV_ITERS + 4

DATA_STEP = 0.5
DUAL_STEP = 0.25
PRIMAL_STEP = 0.25
SMOOTH_WEIGHT = 0.3

MESH = pl.DeviceIdType.MESH
BF16 = jnp.bfloat16
F32 = jnp.float32


def transform_tables(length):
    position = np.arange(length, dtype=np.int64)
    phase_grid = (position[:, None] * position[None, :]) % length
    angles = phase_grid.astype(np.float32) * np.float32(2.0 * np.pi / length)
    norming = np.float32(1.0) / np.sqrt(np.float32(length))
    real_part = (np.cos(angles) * norming).astype(ml_dtypes.bfloat16)
    imag_part = (-np.sin(angles) * norming).astype(ml_dtypes.bfloat16)
    forward_table = np.block([[real_part, -imag_part], [imag_part, real_part]])
    adjoint_table = np.block([[real_part, imag_part], [-imag_part, real_part]])
    return forward_table, adjoint_table


def project(real_part, imag_part):
    factor = jnp.minimum(
        SMOOTH_WEIGHT * lax.rsqrt(real_part * real_part + imag_part * imag_part), 1.0
    )
    return real_part * factor, imag_part * factor


def kernel(
    sizes,
    kspace_hbm, maps_hbm, mask_hbm, image_hbm, forward_hbm, adjoint_hbm,
    image_out, dual_out,
    kspace_raw, maps_raw, kspace_ref, maps_ref, forward_ref, adjoint_ref, masked_ref,
    mask_ref, image_ref, rounded, gathered, coil_data, residual, partial, coded, unit, arrived, units,
    primal, anchor, bar, dual, rim_rows, rim_slices, edges, halo_rows, halo_wide,
    load_sem, first_send, first_recv, start_send, start_recv, ag_send, ag_recv,
    rs_send, rs_recv, unit_send, unit_recv, halo_send, halo_recv, out_send, out_recv,
):
    NR, NCOL, NC, ENC, COIL, CUTS, FRAME = sizes
    ROWS = NR // COIL
    PART = ROWS // FRAME
    LOW = COIL // 4
    WIDE = LOW * FRAME
    BLOCKS = 4 * WIDE
    me = lax.axis_index("coil")
    cut = lax.axis_index("cuts")
    frame = lax.axis_index("frame")
    my_y, my_x = lax.div(me, LOW), frame * LOW + lax.rem(me, LOW)

    def place(y, x):
        return {"coil": y * LOW + lax.rem(x, LOW), "frame": lax.div(x, LOW)}

    def turned(y, x):
        return jnp.where(lax.rem(y, 2) == 0, x, WIDE - 1 - x)

    def block_of(y, x):
        return y * WIDE + turned(y, x)

    def holder(block):
        y = lax.div(block, WIDE)
        return y, turned(y, lax.rem(block, WIDE))

    mine = block_of(my_y, my_x)
    my_block = pl.ds(pl.multiple_of(mine * PART, PART), PART)
    my_rows = pl.ds(pl.multiple_of(me * ROWS, ROWS), ROWS)
    my_place = frame * COIL + me

    offsets = [(dy, dx) for dy in range(4) for dx in range(WIDE) if (dy, dx) != (0, 0)]
    PEERS = len(offsets)
    there = [(lax.rem(my_y + dy, 4), lax.rem(my_x + dx, WIDE)) for dy, dx in offsets]
    origin = [
        (lax.rem(my_y + 4 - dy, 4), lax.rem(my_x + WIDE - dx, WIDE)) for dy, dx in offsets
    ]
    above = place(*holder(lax.rem(mine + BLOCKS - 1, BLOCKS)))
    below = place(*holder(lax.rem(mine + 1, BLOCKS)))
    before, behind = {"cuts": lax.rem(cut + CUTS - 1, CUTS)}, {"cuts": lax.rem(cut + 1, CUTS)}

    def image_load(e, p):
        return pltpu.make_async_copy(
            image_hbm.at[:, p * ENC + e, 0, :], image_ref.at[e, p], load_sem.at[2 * e + p]
        )

    def plain_load(src, dst, i):
        return pltpu.make_async_copy(src, dst, load_sem.at[2 * ENC + i])

    loads = [
        plain_load(maps_hbm, maps_raw, 0),
        plain_load(forward_hbm, forward_ref, 1),
        plain_load(kspace_hbm, kspace_raw, 2),
        plain_load(adjoint_hbm, adjoint_ref, 3),
        plain_load(mask_hbm, mask_ref, 4),
    ]
    for e in range(ENC):
        for p in range(2):
            image_load(e, p).start()
    for load in loads:
        load.start()

    barrier = pltpu.get_barrier_semaphore()
    greeted = [place(*t) for t in there] + [before, behind]
    for other in greeted:
        pl.semaphore_signal(barrier, inc=1, device_id=other, device_id_type=MESH)
    pl.semaphore_wait(barrier, len(greeted))

    def first_copy(e, d):
        other = {"coil": lax.rem(me + 1 + d, COIL)}
        return pltpu.make_async_remote_copy(
            gathered.at[e, :, my_rows, :], gathered.at[e, :, my_rows, :],
            first_send.at[e, d], first_recv.at[e, d], device_id=other, device_id_type=MESH,
        )

    def first_wait(e, d):
        rows = pl.ds(pl.multiple_of(lax.rem(me + COIL - 1 - d, COIL) * ROWS, ROWS), ROWS)
        here = gathered.at[e, :, rows, :]
        pltpu.make_async_remote_copy(
            here, here, first_send.at[e, d], first_recv.at[e, d],
            device_id={"coil": lax.rem(me + 1 + d, COIL)}, device_id_type=MESH,
        ).wait_recv()

    def start_block(k):
        return my_y * WIDE + lax.rem(me, LOW) * FRAME + k

    def start_remote(k):
        return pltpu.make_async_remote_copy(
            image_ref.at[:, :, pl.ds(k * PART, PART), :], primal.at[frame],
            start_send.at[k], start_recv.at[frame],
            device_id=place(*holder(start_block(k))), device_id_type=MESH,
        )

    def start_local(k):
        return pltpu.make_async_copy(
            image_ref.at[:, :, pl.ds(k * PART, PART), :], primal.at[frame], start_send.at[k]
        )

    def ag_copy(e, d):
        return pltpu.make_async_remote_copy(
            rounded.at[e, lax.div(there[d][1], LOW)], gathered.at[e, :, my_block, :],
            ag_send.at[e, d], ag_recv.at[e, d],
            device_id=place(*there[d]), device_id_type=MESH,
        )

    def ag_wait(e, d):
        rows = pl.ds(pl.multiple_of(block_of(*origin[d]) * PART, PART), PART)
        here = gathered.at[e, :, rows, :]
        pltpu.make_async_remote_copy(
            here, here, ag_send.at[e, d], ag_recv.at[e, d],
            device_id=place(*there[d]), device_id_type=MESH,
        ).wait_recv()

    def rs_copy(e, d):
        return pltpu.make_async_remote_copy(
            coded.at[e, block_of(*there[d])], arrived.at[e, my_place],
            rs_send.at[e, d], rs_recv.at[e, d],
            device_id=place(*there[d]), device_id_type=MESH,
        )

    def unit_copy(e, d):
        return pltpu.make_async_remote_copy(
            unit.at[e], units.at[e, my_place], unit_send.at[e, d], unit_recv.at[e, d],
            device_id=place(*there[d]), device_id_type=MESH,
        )

    def halo_copies(e, parity):
        plan = [
            (edges.at[e, 0], halo_rows.at[parity, e, 0], below),
            (edges.at[e, 1], halo_rows.at[parity, e, 1], above),
            (bar.at[e], halo_wide.at[parity, e, 0], behind),
            (bar.at[e], halo_wide.at[parity, e, 1], before),
        ]
        return [
            pltpu.make_async_remote_copy(
                src, dst, halo_send.at[e, i], halo_recv.at[parity, e, i],
                device_id=to, device_id_type=MESH,
            )
            for i, (src, dst, to) in enumerate(plan)
        ]

    my_turn = turned(my_y, my_x)
    my_half = lax.rem(my_turn, FRAME)

    def owner(f):
        return my_y, f * LOW + lax.div(my_turn, FRAME)

    def out_plan(e, f, half):
        rows = pl.ds(pl.multiple_of(half * PART, PART), PART)
        plan = []
        for p in range(2):
            plan.append((primal.at[f, e, p], image_out.at[rows, p * ENC + e, 0, :]))
            for k in range(4):
                plan.append((dual.at[e, k, f, p], dual_out.at[k, rows, p * ENC + e, 0, :]))
        return plan

    def out_remote(e, f):
        return [
            pltpu.make_async_remote_copy(
                src, dst, out_send.at[e, f, i], out_recv.at[e, my_half, i],
                device_id=place(*owner(f)), device_id_type=MESH,
            )
            for i, (src, dst) in enumerate(out_plan(e, f, my_half))
        ]

    def out_local(e, f):
        return [
            pltpu.make_async_copy(src, dst, out_send.at[e, f, i])
            for i, (src, dst) in enumerate(out_plan(e, f, my_half))
        ]

    def out_arrival(e, half):
        return [
            pltpu.make_async_remote_copy(
                dst, dst, out_send.at[e, 0, i], out_recv.at[e, half, i],
                device_id=before, device_id_type=MESH,
            )
            for i, (src, dst) in enumerate(out_plan(e, 0, half))
        ]

    for e in range(ENC):
        for p in range(2):
            image_load(e, p).wait()
            gathered[e, p, my_rows, :] = image_ref[e, p].astype(BF16)
        for d in range(COIL - 1):
            first_copy(e, d).start()
    for k in range(FRAME):
        y, x = holder(start_block(k))

        @pl.when(x != my_x)
        def _():
            start_remote(k).start()

        @pl.when(x == my_x)
        def _():
            start_local(k).start()

    row_id = lax.broadcasted_iota(jnp.int32, (256, 256), 0)
    col_id = lax.broadcasted_iota(jnp.int32, (256, 256), 1)
    source = jnp.where(row_id < 128, 2 * row_id, 2 * row_id - 255)
    sort_rows = jnp.where(col_id == source, 1.0, 0.0).astype(BF16)

    def sorted_pair(block):
        return jnp.dot(
            sort_rows, block.reshape(256, NCOL), preferred_element_type=F32
        ).astype(BF16)

    loads[0].wait()
    for p in range(2):
        def maps_part(i, carry):
            rows = pl.ds(pl.multiple_of(i * 128, 128), 128)
            both = sorted_pair(maps_raw[p, rows])
            maps_ref[p, 0, rows, :] = both[:128]
            maps_ref[p, 1, rows, :] = both[128:]
            return carry

        lax.fori_loop(0, NR // 128, maps_part, 0)
    loads[2].wait()
    for p in range(2):
        def kspace_part(i, carry):
            e, part = lax.rem(i, ENC), lax.div(i, ENC)
            rows = pl.ds(pl.multiple_of(part * 128, 128), 128)
            both = sorted_pair(kspace_raw[p, rows, e])
            kspace_ref[e, p, 0, rows, :] = both[:128]
            kspace_ref[e, p, 1, rows, :] = both[128:]
            return carry

        lax.fori_loop(0, ENC * NR // 128, kspace_part, 0)
    loads[3].wait()
    loads[4].wait()

    def mask_part(i, carry):
        e, part = lax.rem(i, ENC), lax.div(i, ENC)
        rows = pl.ds(pl.multiple_of(part * 64, 64), 64)
        sampled = mask_ref[e].astype(F32)
        for p in range(2):
            columns = pl.ds(p * NR, NR)
            masked_ref[e, rows, columns] = (
                adjoint_ref[rows, columns].astype(F32) * sampled
            ).astype(BF16)
        return carry

    lax.fori_loop(0, ENC * 2 * NR // 64, mask_part, 0)
    dual[...] = jnp.zeros_like(dual)
    rim_rows[...] = jnp.zeros_like(rim_rows)
    rim_slices[...] = jnp.zeros_like(rim_slices)
    edges[...] = jnp.zeros_like(edges)
    loads[1].wait()
    for k in range(FRAME):
        y, x = holder(start_block(k))

        @pl.when(x != my_x)
        def _():
            start_remote(k).wait_send()

        @pl.when(x == my_x)
        def _():
            start_local(k).wait()

    for f in range(FRAME):
        @pl.when(owner(f)[1] != my_x)
        def _():
            pltpu.make_async_remote_copy(
                primal.at[f], primal.at[f], start_send.at[0], start_recv.at[f],
                device_id=before, device_id_type=MESH,
            ).wait_recv()

    def data_stage(e, outer):
        @pl.when(outer == 0)
        def _():
            for d in range(COIL - 1):
                first_wait(e, d)

        @pl.when(outer != 0)
        def _():
            for d in range(PEERS):
                ag_wait(e, d)

        for c in range(NC):
            map_real, map_imag = maps_ref[0, c].astype(F32), maps_ref[1, c].astype(F32)
            image_real, image_imag = gathered[e, 0].astype(F32), gathered[e, 1].astype(F32)
            coil_data[c, :NR] = (map_real * image_real - map_imag * image_imag).astype(BF16)
            coil_data[c, NR:] = (map_real * image_imag + map_imag * image_real).astype(BF16)
            for p in range(2):
                spectrum = jnp.dot(
                    forward_ref[p * NR : (p + 1) * NR], coil_data[c], preferred_element_type=F32
                )
                residual[c, p * NR : (p + 1) * NR] = (
                    spectrum - kspace_ref[e, p, c].astype(F32)
                ).astype(BF16)
        for c in range(NC):
            map_real, map_imag = maps_ref[0, c].astype(F32), maps_ref[1, c].astype(F32)
            back_real = jnp.dot(masked_ref[e, :NR], residual[c], preferred_element_type=F32)
            back_imag = jnp.dot(masked_ref[e, NR:], residual[c], preferred_element_type=F32)
            grad_real = (map_real * back_real + map_imag * back_imag).reshape(BLOCKS, PART, NCOL)
            grad_imag = (map_real * back_imag - map_imag * back_real).reshape(BLOCKS, PART, NCOL)
            if c == 0:
                partial[:, 0], partial[:, 1] = grad_real, grad_imag
            else:
                partial[:, 0] += grad_real
                partial[:, 1] += grad_imag
        top = jnp.max(jnp.abs(partial[...]), axis=(0, 1, 2, 3), keepdims=True)[0, 0]
        step = jnp.broadcast_to(jnp.maximum(top, 1e-30) * (1.0 / 32000.0), (1, NCOL))
        unit[e] = step
        coded[e] = jnp.round(partial[...] * (1.0 / step)).astype(jnp.int32).astype(jnp.int16)
        for d in range(PEERS):
            unit_copy(e, d).start()
            rs_copy(e, d).start()
        units[e, my_place] = step
        arrived[e, my_place] = coded[e, mine]

        @pl.when(outer == 0)
        def _():
            for d in range(COIL - 1):
                first_copy(e, d).wait_send()

        @pl.when(outer != 0)
        def _():
            for d in range(PEERS):
                ag_copy(e, d).wait_send()

    def publish(e, x, parity):
        for f in range(FRAME):
            for p in range(2):
                bar[e, f, p] = x[f][p]
                i = 2 * f + p
                edges[e, 0, i : i + 1, :] = x[f][p][PART - 1 : PART]
                edges[e, 1, i : i + 1, :] = x[f][p][0:1]
        for copy in halo_copies(e, parity):
            copy.start()

    def anchor_stage(e, outer):
        for d in range(PEERS):
            unit_copy(e, d).wait_recv()
            rs_copy(e, d).wait_recv()
        x = [[None, None], [None, None]]
        for f in range(FRAME):
            for p in range(2):
                total = jnp.zeros((PART, NCOL), F32)
                for c in range(f * COIL, f * COIL + COIL):
                    total = total + arrived[e, c, p].astype(F32) * units[e, c]
                x[f][p] = primal[f, e, p] - DATA_STEP * total
                anchor[e, f, p] = x[f][p]
                primal[f, e, p] = x[f][p]
        publish(e, x, lax.rem(outer * TV_ITERS, 2))
        for d in range(PEERS):
            unit_copy(e, d).wait_send()
            rs_copy(e, d).wait_send()

    rows_at = lax.broadcasted_iota(jnp.int32, (PART, NCOL), 0)
    cols_at = lax.broadcasted_iota(jnp.int32, (PART, NCOL), 1)
    last_row = rows_at == PART - 1
    first_row = rows_at == 0
    row_keep = jnp.where(jnp.logical_and(last_row, mine == BLOCKS - 1), 0.0, DUAL_STEP)
    rim_keep = jnp.where(mine == 0, 0.0, 1.0)
    slice_keep = jnp.where(cut == CUTS - 1, 0.0, DUAL_STEP)
    rim_slice_keep = jnp.where(cut == 0, 0.0, 1.0)
    col_keep = jnp.where(cols_at == NCOL - 1, 0.0, DUAL_STEP)
    col_back = jnp.where(cols_at == 0, 0.0, 1.0)

    def tv_stage(e, it, outer):
        parity = lax.rem(outer * TV_ITERS + it, 2)
        for copy in halo_copies(e, parity):
            copy.wait_recv()
        for copy in halo_copies(e, parity):
            copy.wait_send()
        both = [[bar[e, f, p] for p in range(2)] for f in range(FRAME)]
        swing = project(*[
            dual[e, 3, 0, p] + DUAL_STEP * (both[1][p] - both[0][p]) for p in range(2)
        ])
        fresh = [[None, None], [None, None]]
        for p in range(2):
            dual[e, 3, 0, p] = swing[p]
            dual[e, 3, 1, p] = -swing[p]
        for f in range(FRAME):
            x = both[f]

            def stepped(k, diffs):
                new = project(*[dual[e, k, f, p] + diffs[p] for p in range(2)])
                for p in range(2):
                    dual[e, k, f, p] = new[p]
                return new

            after = [halo_rows[parity, e, 1, 2 * f + p : 2 * f + p + 1, :] for p in range(2)]
            prior = [halo_rows[parity, e, 0, 2 * f + p : 2 * f + p + 1, :] for p in range(2)]
            rows = stepped(0, [
                row_keep * (jnp.where(last_row, after[p], pltpu.roll(x[p], PART - 1, 0)) - x[p])
                for p in range(2)
            ])
            rim = project(*[
                rim_rows[e, f, p] + DUAL_STEP * (x[p][0:8] - prior[p]) for p in range(2)
            ])
            spread = [None, None]
            for p in range(2):
                edge = rim[p] * rim_keep
                rim_rows[e, f, p] = edge
                spread[p] = rows[p] - jnp.where(first_row, edge[0:1], pltpu.roll(rows[p], 1, 0))
            cols = stepped(1, [col_keep * (pltpu.roll(x[p], NCOL - 1, 1) - x[p]) for p in range(2)])
            for p in range(2):
                spread[p] = spread[p] + (cols[p] - col_back * pltpu.roll(cols[p], 1, 1))
            cuts = stepped(2, [slice_keep * (halo_wide[parity, e, 1, f, p] - x[p]) for p in range(2)])
            rim = project(*[
                rim_slices[e, f, p] + DUAL_STEP * (x[p] - halo_wide[parity, e, 0, f, p])
                for p in range(2)
            ])
            for p in range(2):
                edge = rim[p] * rim_slice_keep
                rim_slices[e, f, p] = edge
                spread[p] = spread[p] + (cuts[p] - edge)
            for p in range(2):
                spread[p] = spread[p] + (2.0 - 4.0 * f) * swing[p]
                held = primal[f, e, p]
                updated = (held + PRIMAL_STEP * spread[p] + PRIMAL_STEP * anchor[e, f, p]) * (
                    1.0 / (1.0 + PRIMAL_STEP)
                )
                primal[f, e, p] = updated
                fresh[f][p] = 2.0 * updated - held

        @pl.when(it < TV_ITERS - 1)
        def _():
            publish(e, fresh, 1 - parity)

        @pl.when(jnp.logical_and(it == TV_ITERS - 1, outer < OUTER - 1))
        def _():
            for f in range(FRAME):
                for p in range(2):
                    rounded[e, f, p] = primal[f, e, p].astype(BF16)
            for d in range(PEERS):
                ag_copy(e, d).start()
            for p in range(2):
                gathered[e, p, my_block, :] = rounded[e, frame, p]

        @pl.when(jnp.logical_and(it == TV_ITERS - 1, outer == OUTER - 1))
        def _():
            for f in range(FRAME):
                @pl.when(owner(f)[1] != my_x)
                def _():
                    for copy in out_remote(e, f):
                        copy.start()

                @pl.when(owner(f)[1] == my_x)
                def _():
                    for copy in out_local(e, f):
                        copy.start()

    def slot(t, carry):
        def one(i, carry):
            e = ENC - 1 - i
            at = t - e
            outer = lax.div(at, STAGES)
            stage = lax.rem(at, STAGES)
            active = jnp.logical_and(at >= 0, at < OUTER * STAGES)

            @pl.when(jnp.logical_and(active, stage == 0))
            def _():
                data_stage(e, outer)

            @pl.when(jnp.logical_and(active, stage == 2))
            def _():
                anchor_stage(e, outer)

            @pl.when(jnp.logical_and(active, jnp.logical_and(stage >= 3, stage < 3 + TV_ITERS)))
            def _():
                tv_stage(e, stage - 3, outer)

            return carry

        return lax.fori_loop(0, ENC, one, carry)

    lax.fori_loop(0, OUTER * STAGES + ENC - 1, slot, 0)

    def finish(e, carry):
        for f in range(FRAME):
            @pl.when(owner(f)[1] != my_x)
            def _():
                for copy in out_remote(e, f):
                    copy.wait_send()

            @pl.when(owner(f)[1] == my_x)
            def _():
                for copy in out_local(e, f):
                    copy.wait()

        for half in range(FRAME):
            @pl.when(holder(start_block(half))[1] != my_x)
            def _():
                for copy in out_arrival(e, half):
                    copy.wait_recv()

        return carry

    lax.fori_loop(0, ENC, finish, 0)


def solution(mesh):
    COIL, CUTS, FRAME = mesh.shape["coil"], mesh.shape["cuts"], mesh.shape["frame"]

    def shards(kspace, coil_maps, sampling_masks, start_image):
        _, NR, ENC, _, _, NC, NCOL = kspace.shape
        ROWS = start_image.shape[0]
        PART = ROWS // FRAME
        peers = FRAME * COIL - 1
        forward_table, adjoint_table = transform_tables(NR)
        hbm = pl.BlockSpec(memory_space=pltpu.HBM)
        dma = pltpu.SemaphoreType.DMA
        image, dual = pl.pallas_call(
            functools.partial(kernel, (NR, NCOL, NC, ENC, COIL, CUTS, FRAME)),
            out_shape=(
                jax.ShapeDtypeStruct((ROWS, 2 * ENC, 1, NCOL), F32),
                jax.ShapeDtypeStruct((4, ROWS, 2 * ENC, 1, NCOL), F32),
            ),
            in_specs=[hbm] * 6,
            out_specs=(hbm, hbm),
            scratch_shapes=[
                pltpu.VMEM((2, NR, ENC, NC, NCOL), BF16),
                pltpu.VMEM((2, NR, NC, NCOL), BF16),
                pltpu.VMEM((ENC, 2, NC, NR, NCOL), BF16),
                pltpu.VMEM((2, NC, NR, NCOL), BF16),
                pltpu.VMEM((2 * NR, 2 * NR), BF16),
                pltpu.VMEM((2 * NR, 2 * NR), BF16),
                pltpu.VMEM((ENC, 2 * NR, 2 * NR), BF16),
                pltpu.VMEM((ENC, 1, NR), jnp.int32),
                pltpu.VMEM((ENC, 2, ROWS, NCOL), F32),
                pltpu.VMEM((ENC, FRAME, 2, PART, NCOL), BF16),
                pltpu.VMEM((ENC, 2, NR, NCOL), BF16),
                pltpu.VMEM((NC, 2 * NR, NCOL), BF16),
                pltpu.VMEM((NC, 2 * NR, NCOL), BF16),
                pltpu.VMEM((NR // PART, 2, PART, NCOL), F32),
                pltpu.VMEM((ENC, NR // PART, 2, PART, NCOL), jnp.int16),
                pltpu.VMEM((ENC, 1, NCOL), F32),
                pltpu.VMEM((ENC, FRAME * COIL, 2, PART, NCOL), jnp.int16),
                pltpu.VMEM((ENC, FRAME * COIL, 1, NCOL), F32),
                pltpu.VMEM((FRAME, ENC, 2, PART, NCOL), F32),
                pltpu.VMEM((ENC, FRAME, 2, PART, NCOL), F32),
                pltpu.VMEM((ENC, FRAME, 2, PART, NCOL), F32),
                pltpu.VMEM((ENC, 4, FRAME, 2, PART, NCOL), F32),
                pltpu.VMEM((ENC, FRAME, 2, 8, NCOL), F32),
                pltpu.VMEM((ENC, FRAME, 2, PART, NCOL), F32),
                pltpu.VMEM((ENC, 2, 8, NCOL), F32),
                pltpu.VMEM((2, ENC, 2, 8, NCOL), F32),
                pltpu.VMEM((2, ENC, 2, FRAME, 2, PART, NCOL), F32),
                dma((2 * ENC + 5,)),
                dma((ENC, COIL - 1)),
                dma((ENC, COIL - 1)),
                dma((FRAME,)),
                dma((FRAME,)),
                dma((ENC, peers)),
                dma((ENC, peers)),
                dma((ENC, peers)),
                dma((ENC, peers)),
                dma((ENC, peers)),
                dma((ENC, peers)),
                dma((ENC, 4)),
                dma((2, ENC, 4)),
                dma((ENC, FRAME, 10)),
                dma((ENC, FRAME, 10)),
            ],
            compiler_params=pltpu.CompilerParams(
                collective_id=0, has_side_effects=True, vmem_limit_bytes=60 << 20
            ),
            name="sense_tv",
        )(
            kspace.reshape(2, NR, ENC, NC, NCOL),
            coil_maps.reshape(2, NR, NC, NCOL),
            sampling_masks.reshape(ENC, 1, NR),
            start_image.reshape(ROWS, 2 * ENC, 1, NCOL),
            jnp.asarray(forward_table),
            jnp.asarray(adjoint_table),
        )
        return (
            image.reshape(ROWS, 2, ENC, 1, 1, NCOL),
            dual.reshape(4, ROWS, 2, ENC, 1, 1, NCOL),
        )

    return jax.shard_map(
        shards,
        mesh=mesh,
        in_specs=(
            P(None, None, None, "frame", "cuts", "coil", None),
            P(None, None, "cuts", "coil", None),
            P("frame", None, None),
            P("coil", None, None, "frame", "cuts", None),
        ),
        out_specs=(
            P("coil", None, None, "frame", "cuts", None),
            P(None, "coil", None, None, "frame", "cuts", None),
        ),
        check_vma=False,
    )
```

time: 109 us -> 97.9 us (0.90)
  Pallas kernels: 99.5 us -> 92.9 us
  local copies, waits for them, and re-layouts: 7.7 us -> 4.22 us
    pallas_call x1, Pallas kernels: 99.5 us -> 92.9 us  [shards(): pl.pallas_call(functools.partial(kernel, (NR, NCOL, NC, ENC, COIL, CUTS,...]
    unnamed x13 -> x2, local copies, waits for them, and re-layouts: 7.7 us -> 4.22 us
where the time goes in v2:
time: 97.9 us; the launch traced here: 97.7 us
  Pallas kernels  92.9 us (95%)
  local copies, waits for them, and re-layouts  4.22 us (4%)
    pallas_call x1, Pallas kernels, shards(): pl.pallas_call(functools.partial(kernel, (NR, NCOL, NC, ENC, COIL, CUTS,...  92.9 us
    unnamed x2, local copies, waits for them, and re-layouts  4.22 us

profile of v2, /device:TPU:99, one launch (start us, length us, event | category | flops | bytes accessed | tf_op | source)
XLA Modules:
  0.0 97.7 jit_solution(4278704120844640674)
XLA Ops:
  0.6 92.9 %sense_tv.1 = (f32[32,6,1,256]{3,2,1,0:T(1,128)}, f32[4,32,6,1,256]{4,3,2,1,0:T(1,128)}) custom-call(bf16[2,256,3,2,256]{4,3,2,1,0:T(2,128)(2,1)} %bitcast.10, bf16[2,256,2,256]{3,2,1,0:T(2,128)(2,1)} %bitcast.12, s32[3,1,256]{2,1,0:T(1,128)} %bitcast.15, f32[32,6,1,256]{3,2,1,0:T(1,128)} %bitcast.14, bf16[512,512]{1,0:T(8,128)(2,1)} %constant.4.clone.forward_hbm, ...), custom_call_target="tpu_custom_call" | custom-call | tf_op jit(solution)/shard_map/sense_tv/pallas_call | solution.py:558
  93.5 1.7 %copy.12 = f32[32,2,3,1,1,256]{5,4,3,2,1,0:T(1,128)} copy(f32[32,2,3,1,1,256]{5,4,3,2,1,0:T(1,128)} %bitcast.13) | data formatting | bytes 393216
  95.2 2.6 %copy.13 = f32[4,32,2,3,1,1,256]{6,5,4,3,2,1,0:T(1,128)} copy(f32[4,32,2,3,1,1,256]{6,5,4,3,2,1,0:T(1,128)} %bitcast.11) | data formatting | bytes 1572864

commit v3 on v2

--- a/solution.py
+++ b/solution.py
@@ -21,6 +21,8 @@
 MESH = pl.DeviceIdType.MESH
 BF16 = jnp.bfloat16
 F32 = jnp.float32
+I16 = jnp.int16
+CODES = 32000.0
 
 
 def transform_tables(length):
@@ -35,6 +37,10 @@
     return forward_table, adjoint_table
 
 
+def coded_as(values, per_unit):
+    return jnp.round(values * per_unit).astype(jnp.int32).astype(I16)
+
+
 def project(real_part, imag_part):
     factor = jnp.minimum(
         SMOOTH_WEIGHT * lax.rsqrt(real_part * real_part + imag_part * imag_part), 1.0
@@ -45,10 +51,11 @@
 def kernel(
     sizes,
     kspace_hbm, maps_hbm, mask_hbm, image_hbm, forward_hbm, adjoint_hbm,
-    image_out, dual_out,
+    coded_out, unit_out,
     kspace_raw, maps_raw, kspace_ref, maps_ref, forward_ref, adjoint_ref, masked_ref,
     mask_ref, image_ref, rounded, gathered, coil_data, residual, partial, coded, unit, arrived, units,
     primal, anchor, bar, dual, rim_rows, rim_slices, edges, halo_rows, halo_wide,
+    last, last_unit,
     load_sem, first_send, first_recv, start_send, start_recv, ag_send, ag_recv,
     rs_send, rs_recv, unit_send, unit_recv, halo_send, halo_recv, out_send, out_recv,
 ):
@@ -197,28 +204,22 @@
     def owner(f):
         return my_y, f * LOW + lax.div(my_turn, FRAME)
 
-    def out_plan(e, f, half):
-        rows = pl.ds(pl.multiple_of(half * PART, PART), PART)
-        plan = []
-        for p in range(2):
-            plan.append((primal.at[f, e, p], image_out.at[rows, p * ENC + e, 0, :]))
-            for k in range(4):
-                plan.append((dual.at[e, k, f, p], dual_out.at[k, rows, p * ENC + e, 0, :]))
-        return plan
-
     def out_remote(e, f):
+        to = place(*owner(f))
         return [
             pltpu.make_async_remote_copy(
                 src, dst, out_send.at[e, f, i], out_recv.at[e, my_half, i],
-                device_id=place(*owner(f)), device_id_type=MESH,
+                device_id=to, device_id_type=MESH,
             )
-            for i, (src, dst) in enumerate(out_plan(e, f, my_half))
+            for i, (src, dst) in enumerate(
+                [(last.at[e, f], coded_out.at[e, my_half]), (last_unit.at[e], unit_out.at[e, my_half])]
+            )
         ]
 
     def out_local(e, f):
         return [
-            pltpu.make_async_copy(src, dst, out_send.at[e, f, i])
-            for i, (src, dst) in enumerate(out_plan(e, f, my_half))
+            pltpu.make_async_copy(last.at[e, f], coded_out.at[e, my_half], out_send.at[e, f, 0]),
+            pltpu.make_async_copy(last_unit.at[e], unit_out.at[e, my_half], out_send.at[e, f, 1]),
         ]
 
     def out_arrival(e, half):
@@ -227,7 +228,7 @@
                 dst, dst, out_send.at[e, 0, i], out_recv.at[e, half, i],
                 device_id=before, device_id_type=MESH,
             )
-            for i, (src, dst) in enumerate(out_plan(e, 0, half))
+            for i, dst in enumerate([coded_out.at[e, half], unit_out.at[e, half]])
         ]
 
     for e in range(ENC):
@@ -351,10 +352,10 @@
             else:
                 partial[:, 0] += grad_real
                 partial[:, 1] += grad_imag
-        top = jnp.max(jnp.abs(partial[...]), axis=(0, 1, 2, 3), keepdims=True)[0, 0]
-        step = jnp.broadcast_to(jnp.maximum(top, 1e-30) * (1.0 / 32000.0), (1, NCOL))
+        top = jnp.max(jnp.abs(partial[...]), axis=(0, 1, 2), keepdims=True)[0, 0]
+        step = jnp.maximum(top, 1e-30) * (1.0 / CODES)
         unit[e] = step
-        coded[e] = jnp.round(partial[...] * (1.0 / step)).astype(jnp.int32).astype(jnp.int16)
+        coded[e] = coded_as(partial[...], 1.0 / step)
         for d in range(PEERS):
             unit_copy(e, d).start()
             rs_copy(e, d).start()
@@ -484,6 +485,13 @@
 
         @pl.when(jnp.logical_and(it == TV_ITERS - 1, outer == OUTER - 1))
         def _():
+            top = jnp.max(jnp.abs(primal[:, e]), axis=(0, 1, 2), keepdims=True)[0, 0]
+            step = jnp.maximum(top, 1e-30) * (1.0 / CODES)
+            last_unit[e] = step
+            for f in range(FRAME):
+                last[e, f, 4] = coded_as(primal[f, e], 1.0 / step)
+                for k in range(4):
+                    last[e, f, k] = coded_as(dual[e, k, f], CODES / SMOOTH_WEIGHT)
             for f in range(FRAME):
                 @pl.when(owner(f)[1] != my_x)
                 def _():
@@ -542,6 +550,44 @@
         return carry
 
     lax.fori_loop(0, ENC, finish, 0)
+
+
+def restore(coded_hbm, unit_hbm, image_out, dual_out, coded, unit, values, load_sem, out_sem):
+    ENC, FRAME, KINDS, _, PART, NCOL = coded.shape
+    loads = [pltpu.make_async_copy(unit_hbm, unit, load_sem.at[ENC])]
+    loads += [
+        pltpu.make_async_copy(coded_hbm.at[e], coded.at[e], load_sem.at[e]) for e in range(ENC)
+    ]
+    for load in loads:
+        load.start()
+    loads[0].wait()
+
+    def stores(e):
+        copies = []
+        for p in range(2):
+            for k in range(KINDS):
+                if k == KINDS - 1:
+                    to = image_out.at[:, p * ENC + e, 0, :]
+                else:
+                    to = dual_out.at[k, :, p * ENC + e, 0, :]
+                copies.append(
+                    pltpu.make_async_copy(values.at[e, k, p], to, out_sem.at[e, k, p])
+                )
+        return copies
+
+    for e in range(ENC):
+        loads[1 + e].wait()
+        for half in range(FRAME):
+            rows = pl.ds(half * PART, PART)
+            for p in range(2):
+                for k in range(KINDS):
+                    step = unit[e, half] if k == KINDS - 1 else SMOOTH_WEIGHT / CODES
+                    values[e, k, p, rows, :] = coded[e, half, k, p].astype(F32) * step
+        for copy in stores(e):
+            copy.start()
+    for e in range(ENC):
+        for copy in stores(e):
+            copy.wait()
 
 
 def solution(mesh):
@@ -555,11 +601,11 @@
         forward_table, adjoint_table = transform_tables(NR)
         hbm = pl.BlockSpec(memory_space=pltpu.HBM)
         dma = pltpu.SemaphoreType.DMA
-        image, dual = pl.pallas_call(
+        coded, unit = pl.pallas_call(
             functools.partial(kernel, (NR, NCOL, NC, ENC, COIL, CUTS, FRAME)),
             out_shape=(
-                jax.ShapeDtypeStruct((ROWS, 2 * ENC, 1, NCOL), F32),
-                jax.ShapeDtypeStruct((4, ROWS, 2 * ENC, 1, NCOL), F32),
+                jax.ShapeDtypeStruct((ENC, FRAME, 5, 2, PART, NCOL), I16),
+                jax.ShapeDtypeStruct((ENC, FRAME, 1, NCOL), F32),
             ),
             in_specs=[hbm] * 6,
             out_specs=(hbm, hbm),
@@ -578,9 +624,9 @@
                 pltpu.VMEM((NC, 2 * NR, NCOL), BF16),
                 pltpu.VMEM((NC, 2 * NR, NCOL), BF16),
                 pltpu.VMEM((NR // PART, 2, PART, NCOL), F32),
-                pltpu.VMEM((ENC, NR // PART, 2, PART, NCOL), jnp.int16),
+                pltpu.VMEM((ENC, NR // PART, 2, PART, NCOL), I16),
                 pltpu.VMEM((ENC, 1, NCOL), F32),
-                pltpu.VMEM((ENC, FRAME * COIL, 2, PART, NCOL), jnp.int16),
+                pltpu.VMEM((ENC, FRAME * COIL, 2, PART, NCOL), I16),
                 pltpu.VMEM((ENC, FRAME * COIL, 1, NCOL), F32),
                 pltpu.VMEM((FRAME, ENC, 2, PART, NCOL), F32),
                 pltpu.VMEM((ENC, FRAME, 2, PART, NCOL), F32),
@@ -591,6 +637,8 @@
                 pltpu.VMEM((ENC, 2, 8, NCOL), F32),
                 pltpu.VMEM((2, ENC, 2, 8, NCOL), F32),
                 pltpu.VMEM((2, ENC, 2, FRAME, 2, PART, NCOL), F32),
+                pltpu.VMEM((ENC, FRAME, 5, 2, PART, NCOL), I16),
+                pltpu.VMEM((ENC, 1, NCOL), F32),
                 dma((2 * ENC + 5,)),
                 dma((ENC, COIL - 1)),
                 dma((ENC, COIL - 1)),
@@ -604,8 +652,8 @@
                 dma((ENC, peers)),
                 dma((ENC, 4)),
                 dma((2, ENC, 4)),
-                dma((ENC, FRAME, 10)),
-                dma((ENC, FRAME, 10)),
+                dma((ENC, FRAME, 2)),
+                dma((ENC, FRAME, 2)),
             ],
             compiler_params=pltpu.CompilerParams(
                 collective_id=0, has_side_effects=True, vmem_limit_bytes=60 << 20
@@ -619,6 +667,24 @@
             jnp.asarray(forward_table),
             jnp.asarray(adjoint_table),
         )
+        image, dual = pl.pallas_call(
+            restore,
+            out_shape=(
+                jax.ShapeDtypeStruct((ROWS, 2 * ENC, 1, NCOL), F32),
+                jax.ShapeDtypeStruct((4, ROWS, 2 * ENC, 1, NCOL), F32),
+            ),
+            in_specs=[hbm, hbm],
+            out_specs=(hbm, hbm),
+            scratch_shapes=[
+                pltpu.VMEM((ENC, FRAME, 5, 2, PART, NCOL), I16),
+                pltpu.VMEM((ENC, FRAME, 1, NCOL), F32),
+                pltpu.VMEM((ENC, 5, 2, ROWS, NCOL), F32),
+                dma((ENC + 1,)),
+                dma((ENC, 5, 2)),
+            ],
+            compiler_params=pltpu.CompilerParams(vmem_limit_bytes=60 << 20),
+            name="restore",
+        )(coded, unit)
         return (
             image.reshape(ROWS, 2, ENC, 1, 1, NCOL),
             dual.reshape(4, ROWS, 2, ENC, 1, 1, NCOL),

time: 97.9 us -> 85.1 us (0.87)
  Pallas kernels: 92.9 us -> 84.1 us
  local copies, waits for them, and re-layouts: 4.22 us -> 0 us
    pallas_call x1, Pallas kernels: 92.9 us -> 81.9 us  [shards(): pl.pallas_call(functools.partial(kernel, (NR, NCOL, NC, ENC, COIL, CUTS,...]
    unnamed x2 -> x0, local copies, waits for them, and re-layouts: 4.22 us -> none
    pallas_call x0 -> x1, Pallas kernels: none -> 2.19 us  [shards(): pl.pallas_call(restore, out_shape=(jax.ShapeDtypeStruct((ROWS, 2 * ENC, 1...]
where the time goes in v3:
time: 85.1 us; the launch traced here: 84.7 us
  Pallas kernels  84.1 us (99%)
    pallas_call x1, Pallas kernels, shards(): pl.pallas_call(functools.partial(kernel, (NR, NCOL, NC, ENC, COIL, CUTS,...  81.9 us
    pallas_call x1, Pallas kernels, shards(): pl.pallas_call(restore, out_shape=(jax.ShapeDtypeStruct((ROWS, 2 * ENC, 1...  2.19 us

profile of v3, /device:TPU:99, one launch (start us, length us, event | category | flops | bytes accessed | tf_op | source)
XLA Modules:
  0.0 84.7 jit_solution(303793660356459827)
XLA Ops:
  0.6 81.9 %sense_tv.1 = (s16[3,2,5,2,16,256]{5,4,3,2,1,0:T(8,128)(2,1)}, f32[3,2,1,256]{3,2,1,0:T(1,128)}) custom-call(bf16[2,256,3,2,256]{4,3,2,1,0:T(2,128)(2,1)} %bitcast.10, bf16[2,256,2,256]{3,2,1,0:T(2,128)(2,1)} %bitcast.11, s32[3,1,256]{2,1,0:T(1,128)} %bitcast.13, f32[32,6,1,256]{3,2,1,0:T(1,128)} %bitcast.12, bf16[512,512]{1,0:T(8,128)(2,1)} %constant.4.clone.forward_hbm, ...), custom_call_target="tpu_custom_call" | custom-call | tf_op jit(solution)/shard_map/sense_tv/pallas_call | solution.py:604
  82.5 2.2 %restore.1 = (f32[32,6,1,256]{3,2,1,0:T(1,128)}, f32[4,32,6,1,256]{4,3,2,1,0:T(1,128)}) custom-call(s16[3,2,5,2,16,256]{5,4,3,2,1,0:T(8,128)(2,1)} %get-tuple-element.6.coded_hbm, f32[3,2,1,256]{3,2,1,0:T(1,128)} %get-tuple-element.7.unit_hbm), custom_call_target="tpu_custom_call" | custom-call | tf_op jit(solution)/shard_map/restore/pallas_call | solution.py:670

commit v4 on v3

--- a/solution.py
+++ b/solution.py
@@ -91,12 +91,14 @@
     offsets = [(dy, dx) for dy in range(4) for dx in range(WIDE) if (dy, dx) != (0, 0)]
     PEERS = len(offsets)
     there = [(lax.rem(my_y + dy, 4), lax.rem(my_x + dx, WIDE)) for dy, dx in offsets]
-    origin = [
-        (lax.rem(my_y + 4 - dy, 4), lax.rem(my_x + WIDE - dx, WIDE)) for dy, dx in offsets
-    ]
     above = place(*holder(lax.rem(mine + BLOCKS - 1, BLOCKS)))
     below = place(*holder(lax.rem(mine + 1, BLOCKS)))
     before, behind = {"cuts": lax.rem(cut + CUTS - 1, CUTS)}, {"cuts": lax.rem(cut + 1, CUTS)}
+
+    barrier = pltpu.get_barrier_semaphore()
+    greeted = [place(*t) for t in there[::-1]] + [before, behind]
+    for other in greeted:
+        pl.semaphore_signal(barrier, inc=1, device_id=other, device_id_type=MESH)
 
     def image_load(e, p):
         return pltpu.make_async_copy(
@@ -119,26 +121,37 @@
     for load in loads:
         load.start()
 
-    barrier = pltpu.get_barrier_semaphore()
-    greeted = [place(*t) for t in there] + [before, behind]
-    for other in greeted:
-        pl.semaphore_signal(barrier, inc=1, device_id=other, device_id_type=MESH)
+    for e in range(ENC):
+        for p in range(2):
+            image_load(e, p).wait()
+            gathered[e, p, my_rows, :] = image_ref[e, p].astype(BF16)
     pl.semaphore_wait(barrier, len(greeted))
 
     def first_copy(e, d):
         other = {"coil": lax.rem(me + 1 + d, COIL)}
         return pltpu.make_async_remote_copy(
             gathered.at[e, :, my_rows, :], gathered.at[e, :, my_rows, :],
-            first_send.at[e, d], first_recv.at[e, d], device_id=other, device_id_type=MESH,
-        )
-
-    def first_wait(e, d):
-        rows = pl.ds(pl.multiple_of(lax.rem(me + COIL - 1 - d, COIL) * ROWS, ROWS), ROWS)
-        here = gathered.at[e, :, rows, :]
-        pltpu.make_async_remote_copy(
-            here, here, first_send.at[e, d], first_recv.at[e, d],
-            device_id={"coil": lax.rem(me + 1 + d, COIL)}, device_id_type=MESH,
-        ).wait_recv()
+            first_send.at[e], first_recv.at[e], device_id=other, device_id_type=MESH,
+        )
+
+    def all_of(part, send, recv):
+        return pltpu.make_async_remote_copy(
+            part, part, send, recv, device_id=before, device_id_type=MESH
+        )
+
+    def first_all(e):
+        rows = pl.ds(0, (COIL - 1) * ROWS)
+        return all_of(gathered.at[e, :, rows, :], first_send.at[e], first_recv.at[e])
+
+    def ag_all(e):
+        rows = pl.ds(0, PEERS * PART)
+        return all_of(gathered.at[e, :, rows, :], ag_send.at[e], ag_recv.at[e])
+
+    def rs_all(e):
+        return all_of(arrived.at[e, pl.ds(0, PEERS)], rs_send.at[e], rs_recv.at[e])
+
+    def unit_all(e):
+        return all_of(units.at[e, pl.ds(0, PEERS)], unit_send.at[e], unit_recv.at[e])
 
     def start_block(k):
         return my_y * WIDE + lax.rem(me, LOW) * FRAME + k
@@ -158,28 +171,20 @@
     def ag_copy(e, d):
         return pltpu.make_async_remote_copy(
             rounded.at[e, lax.div(there[d][1], LOW)], gathered.at[e, :, my_block, :],
-            ag_send.at[e, d], ag_recv.at[e, d],
+            ag_send.at[e], ag_recv.at[e],
             device_id=place(*there[d]), device_id_type=MESH,
         )
-
-    def ag_wait(e, d):
-        rows = pl.ds(pl.multiple_of(block_of(*origin[d]) * PART, PART), PART)
-        here = gathered.at[e, :, rows, :]
-        pltpu.make_async_remote_copy(
-            here, here, ag_send.at[e, d], ag_recv.at[e, d],
-            device_id=place(*there[d]), device_id_type=MESH,
-        ).wait_recv()
 
     def rs_copy(e, d):
         return pltpu.make_async_remote_copy(
             coded.at[e, block_of(*there[d])], arrived.at[e, my_place],
-            rs_send.at[e, d], rs_recv.at[e, d],
+            rs_send.at[e], rs_recv.at[e],
             device_id=place(*there[d]), device_id_type=MESH,
         )
 
     def unit_copy(e, d):
         return pltpu.make_async_remote_copy(
-            unit.at[e], units.at[e, my_place], unit_send.at[e, d], unit_recv.at[e, d],
+            unit.at[e], units.at[e, my_place], unit_send.at[e], unit_recv.at[e],
             device_id=place(*there[d]), device_id_type=MESH,
         )
 
@@ -232,9 +237,6 @@
         ]
 
     for e in range(ENC):
-        for p in range(2):
-            image_load(e, p).wait()
-            gathered[e, p, my_rows, :] = image_ref[e, p].astype(BF16)
         for d in range(COIL - 1):
             first_copy(e, d).start()
     for k in range(FRAME):
@@ -299,35 +301,14 @@
     rim_slices[...] = jnp.zeros_like(rim_slices)
     edges[...] = jnp.zeros_like(edges)
     loads[1].wait()
-    for k in range(FRAME):
-        y, x = holder(start_block(k))
-
-        @pl.when(x != my_x)
-        def _():
-            start_remote(k).wait_send()
-
-        @pl.when(x == my_x)
-        def _():
-            start_local(k).wait()
-
-    for f in range(FRAME):
-        @pl.when(owner(f)[1] != my_x)
-        def _():
-            pltpu.make_async_remote_copy(
-                primal.at[f], primal.at[f], start_send.at[0], start_recv.at[f],
-                device_id=before, device_id_type=MESH,
-            ).wait_recv()
-
     def data_stage(e, outer):
         @pl.when(outer == 0)
         def _():
-            for d in range(COIL - 1):
-                first_wait(e, d)
+            first_all(e).wait_recv()
 
         @pl.when(outer != 0)
         def _():
-            for d in range(PEERS):
-                ag_wait(e, d)
+            ag_all(e).wait_recv()
 
         for c in range(NC):
             map_real, map_imag = maps_ref[0, c].astype(F32), maps_ref[1, c].astype(F32)
@@ -364,13 +345,11 @@
 
         @pl.when(outer == 0)
         def _():
-            for d in range(COIL - 1):
-                first_copy(e, d).wait_send()
+            first_all(e).wait_send()
 
         @pl.when(outer != 0)
         def _():
-            for d in range(PEERS):
-                ag_copy(e, d).wait_send()
+            ag_all(e).wait_send()
 
     def publish(e, x, parity):
         for f in range(FRAME):
@@ -382,10 +361,30 @@
         for copy in halo_copies(e, parity):
             copy.start()
 
+    def start_wait():
+        for k in range(FRAME):
+            y, x = holder(start_block(k))
+
+            @pl.when(x != my_x)
+            def _():
+                start_remote(k).wait_send()
+
+            @pl.when(x == my_x)
+            def _():
+                start_local(k).wait()
+
+        for f in range(FRAME):
+            @pl.when(owner(f)[1] != my_x)
+            def _():
+                pltpu.make_async_remote_copy(
+                    primal.at[f], primal.at[f], start_send.at[0], start_recv.at[f],
+                    device_id=before, device_id_type=MESH,
+                ).wait_recv()
+
     def anchor_stage(e, outer):
-        for d in range(PEERS):
-            unit_copy(e, d).wait_recv()
-            rs_copy(e, d).wait_recv()
+        pl.when(jnp.logical_and(e == 0, outer == 0))(start_wait)
+        unit_all(e).wait_recv()
+        rs_all(e).wait_recv()
         x = [[None, None], [None, None]]
         for f in range(FRAME):
             for p in range(2):
@@ -396,9 +395,8 @@
                 anchor[e, f, p] = x[f][p]
                 primal[f, e, p] = x[f][p]
         publish(e, x, lax.rem(outer * TV_ITERS, 2))
-        for d in range(PEERS):
-            unit_copy(e, d).wait_send()
-            rs_copy(e, d).wait_send()
+        unit_all(e).wait_send()
+        rs_all(e).wait_send()
 
     rows_at = lax.broadcasted_iota(jnp.int32, (PART, NCOL), 0)
     cols_at = lax.broadcasted_iota(jnp.int32, (PART, NCOL), 1)
@@ -597,7 +595,6 @@
         _, NR, ENC, _, _, NC, NCOL = kspace.shape
         ROWS = start_image.shape[0]
         PART = ROWS // FRAME
-        peers = FRAME * COIL - 1
         forward_table, adjoint_table = transform_tables(NR)
         hbm = pl.BlockSpec(memory_space=pltpu.HBM)
         dma = pltpu.SemaphoreType.DMA
@@ -640,16 +637,16 @@
                 pltpu.VMEM((ENC, FRAME, 5, 2, PART, NCOL), I16),
                 pltpu.VMEM((ENC, 1, NCOL), F32),
                 dma((2 * ENC + 5,)),
-                dma((ENC, COIL - 1)),
-                dma((ENC, COIL - 1)),
+                dma((ENC,)),
+                dma((ENC,)),
                 dma((FRAME,)),
                 dma((FRAME,)),
-                dma((ENC, peers)),
-                dma((ENC, peers)),
-                dma((ENC, peers)),
-                dma((ENC, peers)),
-                dma((ENC, peers)),
-                dma((ENC, peers)),
+                dma((ENC,)),
+                dma((ENC,)),
+                dma((ENC,)),
+                dma((ENC,)),
+                dma((ENC,)),
+                dma((ENC,)),
                 dma((ENC, 4)),
                 dma((2, ENC, 4)),
                 dma((ENC, FRAME, 2)),

time: 85.1 us -> 79.4 us (0.933)
  Pallas kernels: 84.1 us -> 78.2 us
    pallas_call x1, Pallas kernels: 81.9 us -> 76 us  [shards(): pl.pallas_call(functools.partial(kernel, (NR, NCOL, NC, ENC, COIL, CUTS,...]
where the time goes in v4:
time: 79.4 us; the launch traced here: 78.8 us
  Pallas kernels  78.2 us (98%)
    pallas_call x1, Pallas kernels, shards(): pl.pallas_call(functools.partial(kernel, (NR, NCOL, NC, ENC, COIL, CUTS,...  76 us
    pallas_call x1, Pallas kernels, shards(): pl.pallas_call(restore, out_shape=(jax.ShapeDtypeStruct((ROWS, 2 * ENC, 1...  2.19 us

profile of v4, /device:TPU:99, one launch (start us, length us, event | category | flops | bytes accessed | tf_op | source)
XLA Modules:
  0.0 78.8 jit_solution(14030205219388124608)
XLA Ops:
  0.6 76.0 %sense_tv.1 = (s16[3,2,5,2,16,256]{5,4,3,2,1,0:T(8,128)(2,1)}, f32[3,2,1,256]{3,2,1,0:T(1,128)}) custom-call(bf16[2,256,3,2,256]{4,3,2,1,0:T(2,128)(2,1)} %bitcast.10, bf16[2,256,2,256]{3,2,1,0:T(2,128)(2,1)} %bitcast.11, s32[3,1,256]{2,1,0:T(1,128)} %bitcast.13, f32[32,6,1,256]{3,2,1,0:T(1,128)} %bitcast.12, bf16[512,512]{1,0:T(8,128)(2,1)} %constant.4.clone.forward_hbm, ...), custom_call_target="tpu_custom_call" | custom-call | tf_op jit(solution)/shard_map/sense_tv/pallas_call | solution.py:601
  76.6 2.2 %restore.1 = (f32[32,6,1,256]{3,2,1,0:T(1,128)}, f32[4,32,6,1,256]{4,3,2,1,0:T(1,128)}) custom-call(s16[3,2,5,2,16,256]{5,4,3,2,1,0:T(8,128)(2,1)} %get-tuple-element.6.coded_hbm, f32[3,2,1,256]{3,2,1,0:T(1,128)} %get-tuple-element.7.unit_hbm), custom_call_target="tpu_custom_call" | custom-call | tf_op jit(solution)/shard_map/restore/pallas_call | solution.py:667

commit v5 on v4

--- a/solution.py
+++ b/solution.py
@@ -91,12 +91,15 @@
     offsets = [(dy, dx) for dy in range(4) for dx in range(WIDE) if (dy, dx) != (0, 0)]
     PEERS = len(offsets)
     there = [(lax.rem(my_y + dy, 4), lax.rem(my_x + dx, WIDE)) for dy, dx in offsets]
+    places = [place(*t) for t in there]
+    blocks = [block_of(*t) for t in there]
+    frames = [lax.div(x, LOW) for _, x in there]
     above = place(*holder(lax.rem(mine + BLOCKS - 1, BLOCKS)))
     below = place(*holder(lax.rem(mine + 1, BLOCKS)))
     before, behind = {"cuts": lax.rem(cut + CUTS - 1, CUTS)}, {"cuts": lax.rem(cut + 1, CUTS)}
 
     barrier = pltpu.get_barrier_semaphore()
-    greeted = [place(*t) for t in there[::-1]] + [before, behind]
+    greeted = places[::-1] + [before, behind]
     for other in greeted:
         pl.semaphore_signal(barrier, inc=1, device_id=other, device_id_type=MESH)
 
@@ -170,22 +173,22 @@
 
     def ag_copy(e, d):
         return pltpu.make_async_remote_copy(
-            rounded.at[e, lax.div(there[d][1], LOW)], gathered.at[e, :, my_block, :],
+            rounded.at[e, frames[d]], gathered.at[e, :, my_block, :],
             ag_send.at[e], ag_recv.at[e],
-            device_id=place(*there[d]), device_id_type=MESH,
+            device_id=places[d], device_id_type=MESH,
         )
 
     def rs_copy(e, d):
         return pltpu.make_async_remote_copy(
-            coded.at[e, block_of(*there[d])], arrived.at[e, my_place],
+            coded.at[e, blocks[d]], arrived.at[e, my_place],
             rs_send.at[e], rs_recv.at[e],
-            device_id=place(*there[d]), device_id_type=MESH,
+            device_id=places[d], device_id_type=MESH,
         )
 
     def unit_copy(e, d):
         return pltpu.make_async_remote_copy(
             unit.at[e], units.at[e, my_place], unit_send.at[e], unit_recv.at[e],
-            device_id=place(*there[d]), device_id_type=MESH,
+            device_id=places[d], device_id_type=MESH,
         )
 
     def halo_copies(e, parity):
@@ -197,10 +200,16 @@
         ]
         return [
             pltpu.make_async_remote_copy(
-                src, dst, halo_send.at[e, i], halo_recv.at[parity, e, i],
+                src, dst, halo_send.at[e, i // 2], halo_recv.at[parity, e, i // 2],
                 device_id=to, device_id_type=MESH,
             )
             for i, (src, dst, to) in enumerate(plan)
+        ]
+
+    def halo_all(e, parity):
+        return [
+            all_of(part, halo_send.at[e, i], halo_recv.at[parity, e, i])
+            for i, part in enumerate([halo_rows.at[parity, e], halo_wide.at[parity, e]])
         ]
 
     my_turn = turned(my_y, my_x)
@@ -411,9 +420,8 @@
 
     def tv_stage(e, it, outer):
         parity = lax.rem(outer * TV_ITERS + it, 2)
-        for copy in halo_copies(e, parity):
+        for copy in halo_all(e, parity):
             copy.wait_recv()
-        for copy in halo_copies(e, parity):
             copy.wait_send()
         both = [[bar[e, f, p] for p in range(2)] for f in range(FRAME)]
         swing = project(*[
@@ -647,8 +655,8 @@
                 dma((ENC,)),
                 dma((ENC,)),
                 dma((ENC,)),
-                dma((ENC, 4)),
-                dma((2, ENC, 4)),
+                dma((ENC, 2)),
+                dma((2, ENC, 2)),
                 dma((ENC, FRAME, 2)),
                 dma((ENC, FRAME, 2)),
             ],

time: 79.4 us -> 79.2 us (level)
  no operation moved by 1% of the time
where the time goes in v5:
time: 79.2 us; the launch traced here: 78.6 us
  Pallas kernels  78 us (98%)
    pallas_call x1, Pallas kernels, shards(): pl.pallas_call(functools.partial(kernel, (NR, NCOL, NC, ENC, COIL, CUTS,...  75.8 us
    pallas_call x1, Pallas kernels, shards(): pl.pallas_call(restore, out_shape=(jax.ShapeDtypeStruct((ROWS, 2 * ENC, 1...  2.19 us

profile of v5, /device:TPU:99, one launch (start us, length us, event | category | flops | bytes accessed | tf_op | source)
XLA Modules:
  0.0 78.6 jit_solution(15364959663665330480)
XLA Ops:
  0.6 75.8 %sense_tv.1 = (s16[3,2,5,2,16,256]{5,4,3,2,1,0:T(8,128)(2,1)}, f32[3,2,1,256]{3,2,1,0:T(1,128)}) custom-call(bf16[2,256,3,2,256]{4,3,2,1,0:T(2,128)(2,1)} %bitcast.10, bf16[2,256,2,256]{3,2,1,0:T(2,128)(2,1)} %bitcast.11, s32[3,1,256]{2,1,0:T(1,128)} %bitcast.13, f32[32,6,1,256]{3,2,1,0:T(1,128)} %bitcast.12, bf16[512,512]{1,0:T(8,128)(2,1)} %constant.4.clone.forward_hbm, ...), custom_call_target="tpu_custom_call" | custom-call | tf_op jit(solution)/shard_map/sense_tv/pallas_call | solution.py:609
  76.4 2.2 %restore.1 = (f32[32,6,1,256]{3,2,1,0:T(1,128)}, f32[4,32,6,1,256]{4,3,2,1,0:T(1,128)}) custom-call(s16[3,2,5,2,16,256]{5,4,3,2,1,0:T(8,128)(2,1)} %get-tuple-element.6.coded_hbm, f32[3,2,1,256]{3,2,1,0:T(1,128)} %get-tuple-element.7.unit_hbm), custom_call_target="tpu_custom_call" | custom-call | tf_op jit(solution)/shard_map/restore/pallas_call | solution.py:675
